TPU v7x, 32 devices: a whole 2x2x4 slice. The times are simulated.
32 devices in a mesh: ctx: 16 (over z, y, x), fsdp: 2 (over core).
Axes of the slice: x: 2, y: 2, z: 4, core: 2. Of those that a mesh axis runs over, the one named last changes fastest.
Arguments:
- x_in: bfloat16 [4, 1024, 576], P('fsdp', 'ctx')
- w_query: bfloat16 [576, 576], P('fsdp'), may hold values from -0.25 to 0.25
- w_key: bfloat16 [576, 192], P('fsdp'), may hold values from -0.25 to 0.25
- w_value: bfloat16 [576, 192], P('fsdp'), may hold values from -0.25 to 0.25
- w_out: bfloat16 [576, 576], P('fsdp'), may hold values from -6 to 6
- attn_gain: bfloat16 [576], P('fsdp'), may hold values from 0.5 to 1.5
- w_gate: bfloat16 [576, 1536], P('fsdp'), may hold values from -0.25 to 0.25
- w_up: bfloat16 [576, 1536], P('fsdp'), may hold values from -0.25 to 0.25
- w_down: bfloat16 [1536, 576], P('fsdp'), may hold values from -0.15625 to 0.15625
- mlp_gain: bfloat16 [576], P('fsdp'), may hold values from 0.5 to 1.5
- block_of_slot: int32 [32], replicated, may hold values from 0 to 31, as said below
- out_grad: bfloat16 [4, 1024, 576], P('fsdp', 'ctx'), may hold values from -6 to 6
Outputs:
- y_out: bfloat16 [4, 1024, 576], P('fsdp', 'ctx')
- x_grad: bfloat16 [4, 1024, 576], P('fsdp', 'ctx')
- grad_w_query: float32 [576, 576], P('fsdp')
- grad_w_key: float32 [576, 192], P('fsdp')
- grad_w_value: float32 [576, 192], P('fsdp')
- grad_w_out: float32 [576, 576], P('fsdp')
- grad_attn_gain: float32 [576], P('fsdp')
- grad_w_gate: float32 [576, 1536], P('fsdp')
- grad_w_up: float32 [576, 1536], P('fsdp')
- grad_w_down: float32 [1536, 576], P('fsdp')
- grad_mlp_gain: float32 [576], P('fsdp')
Inputs may be any that keep to these rules, and one draw needn't show every extreme that they name: `block_of_slot`: the entries are a permutation of 0 to 31 and entries 2 i and 2 i + 1 sum to 31, so slots 2 i and 2 i + 1 hold a block from the front of the sequence and its mirror from the back.
All inputs are finite; a program needn't handle non-finite values.
Results may differ from a plain program's by a relative error of at most 0.025.
Values may be sent and summed in bfloat16 or wider, within the bound.
A program may use at most 128 MiB of HBM per device.

v0:
```python
import jax
import jax.numpy as jnp
from jax import lax
from jax.sharding import PartitionSpec as P

HEADS = 9
KV_HEADS = 3
HEAD_DIM = 64
epsilon = 1e-05
theta_base = 100000.0
masked_value = -1e30


def shifted(block, axis, distance):
    devices = range(lax.axis_size(axis))
    route = [((i - distance) % len(devices), i) for i in devices]
    return lax.ppermute(block, axis, route)


def make_tables(positions):
    half_dim = HEAD_DIM // 2
    frequency = theta_base ** (-2.0 * jnp.arange(half_dim, dtype=jnp.float32) / HEAD_DIM)
    angles = positions.astype(jnp.float32)[:, None] * frequency[None, :]
    return (jnp.cos(angles), jnp.sin(angles))


def rotate(values, cosine, sine):
    half_dim = values.shape[-1] // 2
    first_half = values[..., :half_dim]
    second_half = values[..., half_dim:]
    cos_rows = cosine[:, None, :]
    sin_rows = sine[:, None, :]
    return jnp.concatenate(
        [
            first_half * cos_rows - second_half * sin_rows,
            second_half * cos_rows + first_half * sin_rows,
        ],
        axis=-1,
    )


def rotate_back(grads, cosine, sine):
    half_dim = grads.shape[-1] // 2
    first_half = grads[..., :half_dim]
    second_half = grads[..., half_dim:]
    cos_rows = cosine[:, None, :]
    sin_rows = sine[:, None, :]
    return jnp.concatenate(
        [
            first_half * cos_rows + second_half * sin_rows,
            second_half * cos_rows - first_half * sin_rows,
        ],
        axis=-1,
    )


def slot_positions(block_of_slot, offset, count_rows, half_len):
    row_ids = offset + jnp.arange(count_rows, dtype=jnp.int32)
    slot_ids = row_ids // half_len
    slot_match = slot_ids[:, None] == jnp.arange(block_of_slot.shape[0], dtype=jnp.int32)[None, :]
    owners = jnp.sum(jnp.where(slot_match, block_of_slot[None, :], 0), axis=1)
    return owners * half_len + row_ids % half_len


def norm_forward(values, gain_vec):
    inverse = lax.rsqrt(jnp.mean(values * values, axis=-1, keepdims=True) + epsilon)
    scaled = values * inverse
    return (scaled * gain_vec, scaled, inverse)


def norm_backward(grad_output, gain_vec, scaled, inverse):
    grad_scaled = grad_output * gain_vec
    grad_input = inverse * (
        grad_scaled - scaled * jnp.mean(grad_scaled * scaled, axis=-1, keepdims=True)
    )
    grad_gain = jnp.sum(grad_output * scaled, axis=0)
    return (grad_input, grad_gain)


def local(
    x_in,
    w_query,
    w_key,
    w_value,
    w_out,
    attn_gain,
    w_gate,
    w_up,
    w_down,
    mlp_gain,
    block_of_slot,
    out_grad,
):
    gathered = (
        lax.all_gather(w_query, "fsdp", axis=0, tiled=True),
        lax.all_gather(w_key, "fsdp", axis=0, tiled=True),
        lax.all_gather(w_value, "fsdp", axis=0, tiled=True),
        lax.all_gather(w_out, "fsdp", axis=0, tiled=True),
        lax.all_gather(attn_gain, "fsdp", axis=0, tiled=True),
        lax.all_gather(w_gate, "fsdp", axis=0, tiled=True),
        lax.all_gather(w_up, "fsdp", axis=0, tiled=True),
        lax.all_gather(w_down, "fsdp", axis=0, tiled=True),
        lax.all_gather(mlp_gain, "fsdp", axis=0, tiled=True),
    )
    (
        full_query,
        full_key,
        full_value,
        full_out,
        gain_attn,
        full_gate,
        full_up,
        full_down,
        gain_mlp,
    ) = gathered
    gain_attn_f = gain_attn.astype(jnp.float32)
    gain_mlp_f = gain_mlp.astype(jnp.float32)
    seq_count, tok_count, model_width = x_in.shape
    group_size = HEADS // KV_HEADS
    half_len = tok_count // 2
    rows_all = seq_count * tok_count
    ctx_count = lax.axis_size("ctx")
    score_scale = HEAD_DIM ** (-0.5)
    my_offset = lax.axis_index("ctx") * tok_count
    query_pos = slot_positions(block_of_slot, my_offset, tok_count, half_len)
    cosine, sine = make_tables(query_pos)
    inputs = x_in.astype(jnp.float32).reshape(rows_all, model_width)
    normed_f, scaled_one, inverse_one = norm_forward(inputs, gain_attn_f)
    normed = normed_f.astype(jnp.bfloat16)
    query_f = jnp.dot(normed, full_query, preferred_element_type=jnp.float32).reshape(
        seq_count, tok_count, HEADS, HEAD_DIM
    )
    queries = (
        rotate(query_f, cosine, sine)
        .astype(jnp.bfloat16)
        .reshape(seq_count, tok_count, KV_HEADS, group_size, HEAD_DIM)
    )
    key_f = jnp.dot(normed, full_key, preferred_element_type=jnp.float32).reshape(
        seq_count, tok_count, KV_HEADS, HEAD_DIM
    )
    key_rows = rotate(key_f, cosine, sine).astype(jnp.bfloat16)
    value_rows = (
        jnp.dot(normed, full_value, preferred_element_type=jnp.float32)
        .astype(jnp.bfloat16)
        .reshape(seq_count, tok_count, KV_HEADS, HEAD_DIM)
    )
    stat_shape = (seq_count, KV_HEADS, group_size, tok_count)
    running_max = jnp.full(stat_shape, masked_value, jnp.float32)
    key_part = lax.all_gather(key_rows, "ctx", axis=1, tiled=True)
    value_part = lax.all_gather(value_rows, "ctx", axis=1, tiled=True)
    key_pos = slot_positions(block_of_slot, jnp.int32(0), key_part.shape[1], half_len)
    visible = query_pos[:, None] >= key_pos[None, :]
    scores = (
        jnp.einsum("sqkgd,snkd->skgqn", queries, key_part, preferred_element_type=jnp.float32)
        * score_scale
    )
    scores = jnp.where(visible, scores, masked_value)
    new_max = jnp.maximum(running_max, jnp.max(scores, axis=-1))
    weights = jnp.where(visible, jnp.exp(scores - new_max[..., None]), 0.0)
    totals = jnp.sum(weights, axis=-1)
    weighted_sum = jnp.einsum(
        "skgqn,snkd->skgqd",
        weights.astype(jnp.bfloat16),
        value_part,
        preferred_element_type=jnp.float32,
    )
    running_max, totals, weighted_sum = (new_max, totals, weighted_sum)
    log_total = running_max + jnp.log(totals)
    attended_f = weighted_sum / totals[..., None]
    attended = (
        attended_f.transpose(0, 3, 1, 2, 4).reshape(rows_all, model_width).astype(jnp.bfloat16)
    )
    hidden_state = inputs + jnp.dot(attended, full_out, preferred_element_type=jnp.float32)
    normed_two_f, scaled_two, inverse_two = norm_forward(hidden_state, gain_mlp_f)
    normed_two = normed_two_f.astype(jnp.bfloat16)
    gate_vals = jnp.dot(normed_two, full_gate, preferred_element_type=jnp.float32)
    up_vals = jnp.dot(normed_two, full_up, preferred_element_type=jnp.float32)
    sigmoid_gate = jax.nn.sigmoid(gate_vals)
    activated = gate_vals * sigmoid_gate
    inner_rows = (activated * up_vals).astype(jnp.bfloat16)
    result = hidden_state + jnp.dot(inner_rows, full_down, preferred_element_type=jnp.float32)
    y_out = result.reshape(seq_count, tok_count, model_width).astype(jnp.bfloat16)
    grad_top = out_grad.reshape(rows_all, model_width)
    grad_residual = grad_top.astype(jnp.float32)
    grad_wdown = jnp.einsum("rf,rd->fd", inner_rows, grad_top, preferred_element_type=jnp.float32)
    grad_inner = jnp.einsum("rd,fd->rf", grad_top, full_down, preferred_element_type=jnp.float32)
    grad_gate = (
        grad_inner * up_vals * sigmoid_gate * (1.0 + gate_vals * (1.0 - sigmoid_gate))
    ).astype(jnp.bfloat16)
    grad_up = (grad_inner * activated).astype(jnp.bfloat16)
    grad_wgate = jnp.einsum("rd,rf->df", normed_two, grad_gate, preferred_element_type=jnp.float32)
    grad_wup = jnp.einsum("rd,rf->df", normed_two, grad_up, preferred_element_type=jnp.float32)
    grad_normed_two = jnp.einsum(
        "rf,df->rd", grad_gate, full_gate, preferred_element_type=jnp.float32
    ) + jnp.einsum("rf,df->rd", grad_up, full_up, preferred_element_type=jnp.float32)
    grad_hidden_norm, grad_gain_mlp = norm_backward(
        grad_normed_two, gain_mlp_f, scaled_two, inverse_two
    )
    grad_hidden = grad_residual + grad_hidden_norm
    grad_branch = grad_hidden.astype(jnp.bfloat16)
    grad_wout = jnp.einsum("ri,rj->ij", attended, grad_branch, preferred_element_type=jnp.float32)
    grad_attended = jnp.einsum(
        "rj,ij->ri", grad_branch, full_out, preferred_element_type=jnp.float32
    ).astype(jnp.bfloat16)
    grad_heads = grad_attended.reshape(
        seq_count, tok_count, KV_HEADS, group_size, HEAD_DIM
    ).transpose(0, 2, 3, 1, 4)
    row_delta = jnp.sum(grad_heads.astype(jnp.float32) * attended_f, axis=-1)

    def block_grads(key_part, value_part, offset):
        key_pos = slot_positions(block_of_slot, offset, key_part.shape[1], half_len)
        visible = query_pos[:, None] >= key_pos[None, :]
        scores = (
            jnp.einsum("sqkgd,snkd->skgqn", queries, key_part, preferred_element_type=jnp.float32)
            * score_scale
        )
        weights = jnp.where(visible, jnp.exp(scores - log_total[..., None]), 0.0)
        grad_value_part = jnp.einsum(
            "skgqn,skgqd->snkd",
            weights.astype(jnp.bfloat16),
            grad_heads,
            preferred_element_type=jnp.float32,
        )
        grad_weights = jnp.einsum(
            "skgqd,snkd->skgqn", grad_heads, value_part, preferred_element_type=jnp.float32
        )
        grad_scores = (weights * (grad_weights - row_delta[..., None])).astype(jnp.bfloat16)
        grad_query_part = jnp.einsum(
            "skgqn,snkd->skgqd", grad_scores, key_part, preferred_element_type=jnp.float32
        )
        grad_key_part = (
            jnp.einsum(
                "skgqn,sqkgd->snkd", grad_scores, queries, preferred_element_type=jnp.float32
            )
            * score_scale
        )
        return (grad_query_part, grad_key_part, grad_value_part)

    grad_query_init = jnp.zeros(stat_shape + (HEAD_DIM,), jnp.float32)
    kv_zero = jnp.zeros(key_rows.shape, jnp.float32)

    def one_hop(hop_index, loop_state):
        key_part, value_part, grad_query, grad_key, grad_value = loop_state
        source = (lax.axis_index("ctx") - hop_index) % ctx_count
        grad_query_part, grad_key_part, grad_value_part = block_grads(
            key_part, value_part, source * tok_count
        )
        key_part, value_part = shifted((key_part, value_part), "ctx", 1)
        grad_key, grad_value = (
            shifted((grad_key + grad_key_part).astype(jnp.bfloat16), "ctx", 1).astype(jnp.float32),
            shifted((grad_value + grad_value_part).astype(jnp.bfloat16), "ctx", 1).astype(
                jnp.float32
            ),
        )
        return (key_part, value_part, grad_query + grad_query_part, grad_key, grad_value)

    loop_state = lax.fori_loop(
        0, ctx_count - 1, one_hop, (key_rows, value_rows, grad_query_init, kv_zero, kv_zero)
    )
    key_part, value_part, grad_query, grad_key, grad_value = loop_state
    source = (lax.axis_index("ctx") + 1) % ctx_count
    grad_query_part, grad_key_part, grad_value_part = block_grads(
        key_part, value_part, source * tok_count
    )
    grad_query = grad_query + grad_query_part
    grad_key, grad_value = (
        shifted((grad_key + grad_key_part).astype(jnp.bfloat16), "ctx", 1).astype(jnp.float32),
        shifted((grad_value + grad_value_part).astype(jnp.bfloat16), "ctx", 1).astype(jnp.float32),
    )
    grad_query_rows = (
        (grad_query * score_scale)
        .transpose(0, 3, 1, 2, 4)
        .reshape(seq_count, tok_count, HEADS, HEAD_DIM)
    )
    grad_query_low = (
        rotate_back(grad_query_rows, cosine, sine)
        .astype(jnp.bfloat16)
        .reshape(rows_all, model_width)
    )
    grad_key_low = (
        rotate_back(grad_key, cosine, sine)
        .astype(jnp.bfloat16)
        .reshape(rows_all, KV_HEADS * HEAD_DIM)
    )
    grad_value_low = grad_value.astype(jnp.bfloat16).reshape(rows_all, KV_HEADS * HEAD_DIM)
    grad_wquery = jnp.einsum(
        "rd,re->de", normed, grad_query_low, preferred_element_type=jnp.float32
    )
    grad_wkey = jnp.einsum("rd,re->de", normed, grad_key_low, preferred_element_type=jnp.float32)
    grad_wvalue = jnp.einsum(
        "rd,re->de", normed, grad_value_low, preferred_element_type=jnp.float32
    )
    grad_normed = jnp.einsum(
        "re,de->rd", grad_query_low, full_query, preferred_element_type=jnp.float32
    )
    grad_normed = grad_normed + jnp.einsum(
        "re,de->rd", grad_key_low, full_key, preferred_element_type=jnp.float32
    )
    grad_normed = grad_normed + jnp.einsum(
        "re,de->rd", grad_value_low, full_value, preferred_element_type=jnp.float32
    )
    grad_input_norm, grad_gain_attn = norm_backward(
        grad_normed, gain_attn_f, scaled_one, inverse_one
    )
    x_grad = (
        (grad_hidden + grad_input_norm)
        .astype(jnp.bfloat16)
        .reshape(seq_count, tok_count, model_width)
    )
    owned_grads = (
        lax.psum_scatter(
            grad_wquery.astype(jnp.bfloat16), "fsdp", scatter_dimension=0, tiled=True
        ).astype(jnp.float32),
        lax.psum_scatter(
            grad_wkey.astype(jnp.bfloat16), "fsdp", scatter_dimension=0, tiled=True
        ).astype(jnp.float32),
        lax.psum_scatter(
            grad_wvalue.astype(jnp.bfloat16), "fsdp", scatter_dimension=0, tiled=True
        ).astype(jnp.float32),
        lax.psum_scatter(
            grad_wout.astype(jnp.bfloat16), "fsdp", scatter_dimension=0, tiled=True
        ).astype(jnp.float32),
        lax.psum_scatter(
            grad_gain_attn.astype(jnp.bfloat16), "fsdp", scatter_dimension=0, tiled=True
        ).astype(jnp.float32),
        lax.psum_scatter(
            grad_wgate.astype(jnp.bfloat16), "fsdp", scatter_dimension=0, tiled=True
        ).astype(jnp.float32),
        lax.psum_scatter(
            grad_wup.astype(jnp.bfloat16), "fsdp", scatter_dimension=0, tiled=True
        ).astype(jnp.float32),
        lax.psum_scatter(
            grad_wdown.astype(jnp.bfloat16), "fsdp", scatter_dimension=0, tiled=True
        ).astype(jnp.float32),
        lax.psum_scatter(
            grad_gain_mlp.astype(jnp.bfloat16), "fsdp", scatter_dimension=0, tiled=True
        ).astype(jnp.float32),
    )
    summed_grads = (
        lax.psum(owned_grads[0].astype(jnp.bfloat16), "ctx").astype(jnp.float32),
        lax.psum(owned_grads[1].astype(jnp.bfloat16), "ctx").astype(jnp.float32),
        lax.psum(owned_grads[2].astype(jnp.bfloat16), "ctx").astype(jnp.float32),
        lax.psum(owned_grads[3].astype(jnp.bfloat16), "ctx").astype(jnp.float32),
        lax.psum(owned_grads[4].astype(jnp.bfloat16), "ctx").astype(jnp.float32),
        lax.psum(owned_grads[5].astype(jnp.bfloat16), "ctx").astype(jnp.float32),
        lax.psum(owned_grads[6].astype(jnp.bfloat16), "ctx").astype(jnp.float32),
        lax.psum(owned_grads[7].astype(jnp.bfloat16), "ctx").astype(jnp.float32),
        lax.psum(owned_grads[8].astype(jnp.bfloat16), "ctx").astype(jnp.float32),
    )
    return (
        y_out,
        x_grad,
        summed_grads[0],
        summed_grads[1],
        summed_grads[2],
        summed_grads[3],
        summed_grads[4],
        summed_grads[5],
        summed_grads[6],
        summed_grads[7],
        summed_grads[8],
    )


def solution(mesh):
    placed = (
        P("fsdp", "ctx", None),
        P("fsdp", None),
        P("fsdp", None),
        P("fsdp", None),
        P("fsdp", None),
        P("fsdp"),
        P("fsdp", None),
        P("fsdp", None),
        P("fsdp", None),
        P("fsdp"),
        P(),
        P("fsdp", "ctx", None),
    )
    return jax.shard_map(
        local,
        mesh=mesh,
        in_specs=placed,
        out_specs=(
            P("fsdp", "ctx", None),
            P("fsdp", "ctx", None),
            P("fsdp", None),
            P("fsdp", None),
            P("fsdp", None),
            P("fsdp", None),
            P("fsdp"),
            P("fsdp", None),
            P("fsdp", None),
            P("fsdp", None),
            P("fsdp"),
        ),
        check_vma=False,
    )
```

profile of v0, /device:TPU:0, one launch (start us, length us, event | category | flops | bytes accessed | tf_op | source)
XLA Modules:
  0.0 655.3 jit_solution(17104645423890764450)
XLA Ops:
  12.6 2.6 all-reduce.7
  15.5 2.0 all_gather.34
  18.4 54.9 %all_gather.35 = bf16[2,1024,3,64]{3,0,2,1:T(2,128)(2,1)} all-gather(bf16[2,64,3,64]{3,0,2,1:T(2,128)(2,1)S(1)} %copy.115), channel_id=1, replica_groups=mesh['ctx'=16,'fsdp'=2] {'ctx'}, dimensions={1}, use_global_device_ids=true | all-gather | bytes 835584 | tf_op jit(solution)/shard_map/all_gather | solution.py:149
  73.3 2.3 all_gather.36
  78.7 3.1 fusion.17
  81.9 2.0 all_gather.37
  84.5 49.6 %all_gather.38 = bf16[2,1024,3,64]{3,0,2,1:T(2,128)(2,1)S(1)} all-gather(bf16[2,64,3,64]{3,0,2,1:T(2,128)(2,1)S(1)} %copy.121), channel_id=1, replica_groups=mesh['ctx'=16,'fsdp'=2] {'ctx'}, dimensions={1}, use_global_device_ids=true | all-gather | bytes 835584 | tf_op jit(solution)/shard_map/all_gather | solution.py:150
  134.2 3.9 fusion.18
  138.1 2.5 fusion.41
  141.1 2.5 all_gather.39
  146.6 1.3 broadcast_compare_fusion.2
  148.8 2.9 fusion.74
  151.7 2.9 fusion.75
  154.5 3.5 multiply_convert_fusion
  163.3 216.1 %while.25 = (s32[]{:T(128)}, bf16[2,64,3,64]{3,1,2,0:T(8,128)(2,1)S(1)}, bf16[2,64,3,64]{3,1,2,0:T(8,128)(2,1)S(1)}, f32[2,3,3,64,64]{4,3,2,1,0:T(8,128)S(1)}, f...) while((s32[]{:T(128)}, ...), condition=%wide.region_10.11_spmd.clone, body=%wide.region_8.10_spmd.clone.sunk | while | flops 48082768 | bytes 4246918 | solution.py:257
  168.7 8.0 %collective-permute-done.2 = bf16[2,64,3,64]{3,1,2,0:T(8,128)(2,1)S(1)} collective-permute-done((bf16[2,64,3,64]{3,1,2,0:T(8,128)(2,1)S(1)}, bf16[2,64,3,64]{3,1,2,0:T(8,128)(2,1)S(1)}, u32[]{:S(2)}, u32[]{:S(2)}) %collective-permute-start.2) | collective-permute-done | bytes 49184 | tf_op jit(solution)/shard_map/while/body/eval_jaxpr/ppermute | solution.py:17
  176.7 1.4 collective-permute-done.3
  182.3 8.6 %collective-permute-done.2 = bf16[2,64,3,64]{3,1,2,0:T(8,128)(2,1)S(1)} collective-permute-done((bf16[2,64,3,64]{3,1,2,0:T(8,128)(2,1)S(1)}, bf16[2,64,3,64]{3,1,2,0:T(8,128)(2,1)S(1)}, u32[]{:S(2)}, u32[]{:S(2)}) %collective-permute-start.2) | collective-permute-done | bytes 49184 | tf_op jit(solution)/shard_map/while/body/eval_jaxpr/ppermute | solution.py:17
  190.9 1.3 collective-permute-done.3
  196.1 2.8 collective-permute-start.3
  199.3 5.9 collective-permute-done.2
  206.5 1.6 collective-permute-start.1
  211.7 2.2 collective-permute-start.3
  214.3 5.3 collective-permute-done.2
  225.8 2.1 collective-permute-start.3
  228.3 5.3 collective-permute-done.2
  238.9 4.3 collective-permute-start.3
  243.6 3.4 collective-permute-done.2
  248.3 3.4 collective-permute-start.1
  255.6 2.3 collective-permute-start.3
  258.3 4.9 collective-permute-done.2
  269.1 1.8 collective-permute-start.3
  271.3 5.8 collective-permute-done.2
  277.0 1.8 collective-permute-done.3
  283.1 2.1 collective-permute-start.3
  285.5 6.4 collective-permute-done.2
  292.0 1.9 collective-permute-done.3
  297.7 3.1 collective-permute-start.3
  301.2 6.1 collective-permute-done.2
  307.3 2.1 collective-permute-done.3
  314.8 8.1 %collective-permute-done.2 = bf16[2,64,3,64]{3,1,2,0:T(8,128)(2,1)S(1)} collective-permute-done((bf16[2,64,3,64]{3,1,2,0:T(8,128)(2,1)S(1)}, bf16[2,64,3,64]{3,1,2,0:T(8,128)(2,1)S(1)}, u32[]{:S(2)}, u32[]{:S(2)}) %collective-permute-start.2) | collective-permute-done | bytes 49184 | tf_op jit(solution)/shard_map/while/body/eval_jaxpr/ppermute | solution.py:17
  322.9 1.3 collective-permute-done.3
  328.5 8.6 %collective-permute-done.2 = bf16[2,64,3,64]{3,1,2,0:T(8,128)(2,1)S(1)} collective-permute-done((bf16[2,64,3,64]{3,1,2,0:T(8,128)(2,1)S(1)}, bf16[2,64,3,64]{3,1,2,0:T(8,128)(2,1)S(1)}, u32[]{:S(2)}, u32[]{:S(2)}) %collective-permute-start.2) | collective-permute-done | bytes 49184 | tf_op jit(solution)/shard_map/while/body/eval_jaxpr/ppermute | solution.py:17
  342.2 2.0 collective-permute-start.3
  344.6 6.6 %collective-permute-done.2 = bf16[2,64,3,64]{3,1,2,0:T(8,128)(2,1)S(1)} collective-permute-done((bf16[2,64,3,64]{3,1,2,0:T(8,128)(2,1)S(1)}, bf16[2,64,3,64]{3,1,2,0:T(8,128)(2,1)S(1)}, u32[]{:S(2)}, u32[]{:S(2)}) %collective-permute-start.2) | collective-permute-done | bytes 49184 | tf_op jit(solution)/shard_map/while/body/eval_jaxpr/ppermute | solution.py:17
  357.6 7.6 %collective-permute-done.2 = bf16[2,64,3,64]{3,1,2,0:T(8,128)(2,1)S(1)} collective-permute-done((bf16[2,64,3,64]{3,1,2,0:T(8,128)(2,1)S(1)}, bf16[2,64,3,64]{3,1,2,0:T(8,128)(2,1)S(1)}, u32[]{:S(2)}, u32[]{:S(2)}) %collective-permute-start.2) | collective-permute-done | bytes 49184 | tf_op jit(solution)/shard_map/while/body/eval_jaxpr/ppermute | solution.py:17
  370.4 2.6 collective-permute-start.3
  373.3 5.0 collective-permute-done.2
  381.8 7.3 %collective-permute-done.5 = bf16[2,64,3,64]{1,3,2,0:T(8,128)(2,1)S(1)} collective-permute-done((bf16[2,64,3,64]{1,3,2,0:T(8,128)(2,1)S(1)}, bf16[2,64,3,64]{1,3,2,0:T(8,128)(2,1)S(1)}, u32[]{:S(2)}, u32[]{:S(2)}) %collective-permute-start.5) | collective-permute-done | bytes 49184 | tf_op jit(solution)/shard_map/ppermute | solution.py:17
  395.6 1.8 convolution_convert_fusion.1
  397.5 1.8 convolution_convert_fusion.2
  399.4 1.9 convolution_convert_fusion
  401.6 3.7 reduce-scatter.10.cloned.1.call-done
  405.3 11.5 %reduce-scatter.14.cloned.1.call-done = bf16[288,576]{1,0:T(8,128)(2,1)} async-done(((bf16[576,576]{1,0:T(8,128)(2,1)}), bf16[288,576]{1,0:T(8,128)(2,1)}) %reduce-scatter.14.cloned.1.call-update) | async-done | bytes 331792 | tf_op jit(solution)/shard_map/reduce_scatter | solution.py:320
  416.8 12.2 %reduce-scatter.8.cloned.1.call-done = bf16[288,576]{1,0:T(8,128)(2,1)} async-done(((bf16[576,576]{1,0:T(8,128)(2,1)}), bf16[288,576]{1,0:T(8,128)(2,1)}) %reduce-scatter.8.cloned.1.call-update) | async-done | bytes 331792 | tf_op jit(solution)/shard_map/reduce_scatter | solution.py:311
  429.0 13.3 %reduce-scatter.18.cloned.1.call-done = bf16[288,1536]{1,0:T(8,128)(2,1)} async-done(((bf16[576,1536]{1,0:T(8,128)(2,1)}), bf16[288,1536]{1,0:T(8,128)(2,1)}) %reduce-scatter.18.cloned.1.call-update) | async-done | bytes 884752 | tf_op jit(solution)/shard_map/reduce_scatter | solution.py:329
  442.4 13.4 %reduce-scatter.16.cloned.1.call-done = bf16[288,1536]{1,0:T(8,128)(2,1)} async-done(((bf16[576,1536]{1,0:T(8,128)(2,1)}), bf16[288,1536]{1,0:T(8,128)(2,1)}) %reduce-scatter.16.cloned.1.call-update) | async-done | bytes 884752 | tf_op jit(solution)/shard_map/reduce_scatter | solution.py:326
  455.8 13.2 %reduce-scatter.20.cloned.1.call-done = bf16[768,576]{0,1:T(8,128)(2,1)} async-done(((bf16[1536,576]{0,1:T(8,128)(2,1)}), bf16[768,576]{0,1:T(8,128)(2,1)}) %reduce-scatter.20.cloned.1.call-update) | async-done | bytes 884752 | tf_op jit(solution)/shard_map/reduce_scatter | solution.py:332
  469.7 2.1 fusion.33
  473.7 2.5 all-reduce.6
  476.4 43.7 %all-reduce.4 = (bf16[288]{0:T(512)(128)(2,1)S(1)}, bf16[288]{0:T(512)(128)(2,1)S(1)}) all-reduce(bf16[288]{0:T(512)(128)(2,1)S(1)} %dynamic-slice.3, bf16[288]{0:T(512)(128)(2,1)S(1)} %dynamic-slice.5), channel_id=1, replica_groups=mesh['ctx'=16,'fsdp'=2] {'ctx'}, use_global_device_ids=true, to_apply=%region_23.24 | all-reduce | flops 576 | bytes 2304 | tf_op jit(solution)/shard_map/psum | solution.py:344
  522.2 117.8 %all-reduce.10.cloned.1.call-done = (bf16[288,576]{1,0:T(8,128)(2,1)}, bf16[288,192]{1,0:T(8,128)(2,1)}, bf16[288,192]{1,0:T(8,128)(2,1)}, bf16[288,576]{1,0:T(8...) async-done(((bf16[288,576]{1,0:T(8,128)(2,1)}, bf16[288,192]{1,0:T(8,128)(2,1)}, bf16[288,192]{1,0:T(8,128)(2,1)}, ...) | async-done | bytes 3538960 | tf_op jit(solution)/shard_map/psum | solution.py:340
  640.0 2.7 convert_element_type.301
  642.7 1.4 convert_element_type.303
  (509 shorter events, 114.7 us)
Async XLA Ops:
  7.2 141.5 %all-gather.4.cloned.1.call-start = ((), (), s32[]{:S(2)}) async-start(), calls=%async_computation.7 | async-start | bytes 2654208 | tf_op jit(solution)/shard_map/all_gather | solution.py:100
  8.0 143.7 %all-gather.6.cloned.1.call-start = ((), (), s32[]{:S(2)}) async-start(), calls=%async_computation.8 | async-start | bytes 2654208 | tf_op jit(solution)/shard_map/all_gather | solution.py:101
  8.7 145.8 %all-gather.8.cloned.1.call-start = ((), (), s32[]{:S(2)}) async-start(), calls=%async_computation.9 | async-start | bytes 2654208 | tf_op jit(solution)/shard_map/all_gather | solution.py:102
  9.4 392.2 %reduce-scatter.12.cloned.1.call-start = ((), (), s32[]{:S(2)}) async-start(), calls=%async_computation.12 | async-start | bytes 442368 | tf_op jit(solution)/shard_map/reduce_scatter | solution.py:317
  163.3 14.8 %collective-permute-start = (bf16[2,64,3,64]{3,1,2,0:T(8,128)(2,1)S(1)}, bf16[2,64,3,64]{3,1,2,0:T(8,128)(2,1)S(1)}, u32[]{:S(2)}, u32[]{:S(2)}) collective-permute-start(bf16[2,64,3,64]{3,1,2,0:T(8,128)(2,1)S(1)} %copy.200), channel_id=1, source_target_pairs={{30,0},{0,2},{2,4},{4,6},{6,8},{8,10},{10,12},{12,14},{14,16},{16,... | collective-permute-start | bytes 147464 | tf_op jit(solution)/shard_map/while/body/eval_jaxpr/ppermute | solution.py:17
  164.0 14.1 %collective-permute-start.1 = (bf16[2,64,3,64]{3,1,2,0:T(8,128)(2,1)S(1)}, bf16[2,64,3,64]{3,1,2,0:T(8,128)(2,1)S(1)}, u32[]{:S(2)}, u32[]{:S(2)}) collective-permute-start(bf16[2,64,3,64]{3,1,2,0:T(8,128)(2,1)S(1)} %copy.201), channel_id=1, source_target_pairs={{30,0},{0,2},{2,4},{4,6},{6,8},{8,10},{10,12},{12,14},{14,16},{16,... | collective-permute-start | bytes 147464 | tf_op jit(solution)/shard_map/while/body/eval_jaxpr/ppermute | solution.py:17
  167.3 9.3 %collective-permute-start.2 = (bf16[2,64,3,64]{3,1,2,0:T(8,128)(2,1)S(1)}, bf16[2,64,3,64]{3,1,2,0:T(8,128)(2,1)S(1)}, u32[]{:S(2)}, u32[]{:S(2)}) collective-permute-start(bf16[2,64,3,64]{3,1,2,0:T(8,128)(2,1)S(1)} %fusion.154), channel_id=1, source_target_pairs={{30,0},{0,2},{2,4},{4,6},{6,8},{8,10},{10,12},{12,14},{14,16},{16,... | collective-permute-start | bytes 147464 | tf_op jit(solution)/shard_map/while/body/eval_jaxpr/ppermute | solution.py:17
  167.7 10.4 %collective-permute-start.3 = (bf16[2,64,3,64]{3,1,2,0:T(8,128)(2,1)S(1)}, bf16[2,64,3,64]{3,1,2,0:T(8,128)(2,1)S(1)}, u32[]{:S(2)}, u32[]{:S(2)}) collective-permute-start(bf16[2,64,3,64]{3,1,2,0:T(8,128)(2,1)S(1)} %fusion.155), channel_id=1, source_target_pairs={{30,0},{0,2},{2,4},{4,6},{6,8},{8,10},{10,12},{12,14},{14,16},{16,... | collective-permute-start | bytes 147464 | tf_op jit(solution)/shard_map/while/body/eval_jaxpr/ppermute | solution.py:17
  178.2 14.1 %collective-permute-start = (bf16[2,64,3,64]{3,1,2,0:T(8,128)(2,1)S(1)}, bf16[2,64,3,64]{3,1,2,0:T(8,128)(2,1)S(1)}, u32[]{:S(2)}, u32[]{:S(2)}) collective-permute-start(bf16[2,64,3,64]{3,1,2,0:T(8,128)(2,1)S(1)} %copy.200), channel_id=1, source_target_pairs={{30,0},{0,2},{2,4},{4,6},{6,8},{8,10},{10,12},{12,14},{14,16},{16,... | collective-permute-start | bytes 147464 | tf_op jit(solution)/shard_map/while/body/eval_jaxpr/ppermute | solution.py:17
  178.2 14.1 %collective-permute-start.1 = (bf16[2,64,3,64]{3,1,2,0:T(8,128)(2,1)S(1)}, bf16[2,64,3,64]{3,1,2,0:T(8,128)(2,1)S(1)}, u32[]{:S(2)}, u32[]{:S(2)}) collective-permute-start(bf16[2,64,3,64]{3,1,2,0:T(8,128)(2,1)S(1)} %copy.201), channel_id=1, source_target_pairs={{30,0},{0,2},{2,4},{4,6},{6,8},{8,10},{10,12},{12,14},{14,16},{16,... | collective-permute-start | bytes 147464 | tf_op jit(solution)/shard_map/while/body/eval_jaxpr/ppermute | solution.py:17
  181.6 9.3 %collective-permute-start.2 = (bf16[2,64,3,64]{3,1,2,0:T(8,128)(2,1)S(1)}, bf16[2,64,3,64]{3,1,2,0:T(8,128)(2,1)S(1)}, u32[]{:S(2)}, u32[]{:S(2)}) collective-permute-start(bf16[2,64,3,64]{3,1,2,0:T(8,128)(2,1)S(1)} %fusion.154), channel_id=1, source_target_pairs={{30,0},{0,2},{2,4},{4,6},{6,8},{8,10},{10,12},{12,14},{14,16},{16,... | collective-permute-start | bytes 147464 | tf_op jit(solution)/shard_map/while/body/eval_jaxpr/ppermute | solution.py:17
  181.9 10.4 %collective-permute-start.3 = (bf16[2,64,3,64]{3,1,2,0:T(8,128)(2,1)S(1)}, bf16[2,64,3,64]{3,1,2,0:T(8,128)(2,1)S(1)}, u32[]{:S(2)}, u32[]{:S(2)}) collective-permute-start(bf16[2,64,3,64]{3,1,2,0:T(8,128)(2,1)S(1)} %fusion.155), channel_id=1, source_target_pairs={{30,0},{0,2},{2,4},{4,6},{6,8},{8,10},{10,12},{12,14},{14,16},{16,... | collective-permute-start | bytes 147464 | tf_op jit(solution)/shard_map/while/body/eval_jaxpr/ppermute | solution.py:17
  192.4 14.1 %collective-permute-start = (bf16[2,64,3,64]{3,1,2,0:T(8,128)(2,1)S(1)}, bf16[2,64,3,64]{3,1,2,0:T(8,128)(2,1)S(1)}, u32[]{:S(2)}, u32[]{:S(2)}) collective-permute-start(bf16[2,64,3,64]{3,1,2,0:T(8,128)(2,1)S(1)} %copy.200), channel_id=1, source_target_pairs={{30,0},{0,2},{2,4},{4,6},{6,8},{8,10},{10,12},{12,14},{14,16},{16,... | collective-permute-start | bytes 147464 | tf_op jit(solution)/shard_map/while/body/eval_jaxpr/ppermute | solution.py:17
  192.4 14.0 %collective-permute-start.1 = (bf16[2,64,3,64]{3,1,2,0:T(8,128)(2,1)S(1)}, bf16[2,64,3,64]{3,1,2,0:T(8,128)(2,1)S(1)}, u32[]{:S(2)}, u32[]{:S(2)}) collective-permute-start(bf16[2,64,3,64]{3,1,2,0:T(8,128)(2,1)S(1)} %copy.201), channel_id=1, source_target_pairs={{30,0},{0,2},{2,4},{4,6},{6,8},{8,10},{10,12},{12,14},{14,16},{16,... | collective-permute-start | bytes 147464 | tf_op jit(solution)/shard_map/while/body/eval_jaxpr/ppermute | solution.py:17
  195.8 9.4 %collective-permute-start.2 = (bf16[2,64,3,64]{3,1,2,0:T(8,128)(2,1)S(1)}, bf16[2,64,3,64]{3,1,2,0:T(8,128)(2,1)S(1)}, u32[]{:S(2)}, u32[]{:S(2)}) collective-permute-start(bf16[2,64,3,64]{3,1,2,0:T(8,128)(2,1)S(1)} %fusion.154), channel_id=1, source_target_pairs={{30,0},{0,2},{2,4},{4,6},{6,8},{8,10},{10,12},{12,14},{14,16},{16,... | collective-permute-start | bytes 147464 | tf_op jit(solution)/shard_map/while/body/eval_jaxpr/ppermute | solution.py:17
  196.1 10.3 %collective-permute-start.3 = (bf16[2,64,3,64]{3,1,2,0:T(8,128)(2,1)S(1)}, bf16[2,64,3,64]{3,1,2,0:T(8,128)(2,1)S(1)}, u32[]{:S(2)}, u32[]{:S(2)}) collective-permute-start(bf16[2,64,3,64]{3,1,2,0:T(8,128)(2,1)S(1)} %fusion.155), channel_id=1, source_target_pairs={{30,0},{0,2},{2,4},{4,6},{6,8},{8,10},{10,12},{12,14},{14,16},{16,... | collective-permute-start | bytes 147464 | tf_op jit(solution)/shard_map/while/body/eval_jaxpr/ppermute | solution.py:17
  206.5 14.2 %collective-permute-start = (bf16[2,64,3,64]{3,1,2,0:T(8,128)(2,1)S(1)}, bf16[2,64,3,64]{3,1,2,0:T(8,128)(2,1)S(1)}, u32[]{:S(2)}, u32[]{:S(2)}) collective-permute-start(bf16[2,64,3,64]{3,1,2,0:T(8,128)(2,1)S(1)} %copy.200), channel_id=1, source_target_pairs={{30,0},{0,2},{2,4},{4,6},{6,8},{8,10},{10,12},{12,14},{14,16},{16,... | collective-permute-start | bytes 147464 | tf_op jit(solution)/shard_map/while/body/eval_jaxpr/ppermute | solution.py:17
  206.5 14.2 %collective-permute-start.1 = (bf16[2,64,3,64]{3,1,2,0:T(8,128)(2,1)S(1)}, bf16[2,64,3,64]{3,1,2,0:T(8,128)(2,1)S(1)}, u32[]{:S(2)}, u32[]{:S(2)}) collective-permute-start(bf16[2,64,3,64]{3,1,2,0:T(8,128)(2,1)S(1)} %copy.201), channel_id=1, source_target_pairs={{30,0},{0,2},{2,4},{4,6},{6,8},{8,10},{10,12},{12,14},{14,16},{16,... | collective-permute-start | bytes 147464 | tf_op jit(solution)/shard_map/while/body/eval_jaxpr/ppermute | solution.py:17
  211.7 8.9 %collective-permute-start.3 = (bf16[2,64,3,64]{3,1,2,0:T(8,128)(2,1)S(1)}, bf16[2,64,3,64]{3,1,2,0:T(8,128)(2,1)S(1)}, u32[]{:S(2)}, u32[]{:S(2)}) collective-permute-start(bf16[2,64,3,64]{3,1,2,0:T(8,128)(2,1)S(1)} %fusion.155), channel_id=1, source_target_pairs={{30,0},{0,2},{2,4},{4,6},{6,8},{8,10},{10,12},{12,14},{14,16},{16,... | collective-permute-start | bytes 147464 | tf_op jit(solution)/shard_map/while/body/eval_jaxpr/ppermute | solution.py:17
  220.8 13.8 %collective-permute-start = (bf16[2,64,3,64]{3,1,2,0:T(8,128)(2,1)S(1)}, bf16[2,64,3,64]{3,1,2,0:T(8,128)(2,1)S(1)}, u32[]{:S(2)}, u32[]{:S(2)}) collective-permute-start(bf16[2,64,3,64]{3,1,2,0:T(8,128)(2,1)S(1)} %copy.200), channel_id=1, source_target_pairs={{30,0},{0,2},{2,4},{4,6},{6,8},{8,10},{10,12},{12,14},{14,16},{16,... | collective-permute-start | bytes 147464 | tf_op jit(solution)/shard_map/while/body/eval_jaxpr/ppermute | solution.py:17
  220.8 13.8 %collective-permute-start.1 = (bf16[2,64,3,64]{3,1,2,0:T(8,128)(2,1)S(1)}, bf16[2,64,3,64]{3,1,2,0:T(8,128)(2,1)S(1)}, u32[]{:S(2)}, u32[]{:S(2)}) collective-permute-start(bf16[2,64,3,64]{3,1,2,0:T(8,128)(2,1)S(1)} %copy.201), channel_id=1, source_target_pairs={{30,0},{0,2},{2,4},{4,6},{6,8},{8,10},{10,12},{12,14},{14,16},{16,... | collective-permute-start | bytes 147464 | tf_op jit(solution)/shard_map/while/body/eval_jaxpr/ppermute | solution.py:17
  225.8 8.8 %collective-permute-start.3 = (bf16[2,64,3,64]{3,1,2,0:T(8,128)(2,1)S(1)}, bf16[2,64,3,64]{3,1,2,0:T(8,128)(2,1)S(1)}, u32[]{:S(2)}, u32[]{:S(2)}) collective-permute-start(bf16[2,64,3,64]{3,1,2,0:T(8,128)(2,1)S(1)} %fusion.155), channel_id=1, source_target_pairs={{30,0},{0,2},{2,4},{4,6},{6,8},{8,10},{10,12},{12,14},{14,16},{16,... | collective-permute-start | bytes 147464 | tf_op jit(solution)/shard_map/while/body/eval_jaxpr/ppermute | solution.py:17
  234.7 13.4 %collective-permute-start = (bf16[2,64,3,64]{3,1,2,0:T(8,128)(2,1)S(1)}, bf16[2,64,3,64]{3,1,2,0:T(8,128)(2,1)S(1)}, u32[]{:S(2)}, u32[]{:S(2)}) collective-permute-start(bf16[2,64,3,64]{3,1,2,0:T(8,128)(2,1)S(1)} %copy.200), channel_id=1, source_target_pairs={{30,0},{0,2},{2,4},{4,6},{6,8},{8,10},{10,12},{12,14},{14,16},{16,... | collective-permute-start | bytes 147464 | tf_op jit(solution)/shard_map/while/body/eval_jaxpr/ppermute | solution.py:17
  234.7 13.3 %collective-permute-start.1 = (bf16[2,64,3,64]{3,1,2,0:T(8,128)(2,1)S(1)}, bf16[2,64,3,64]{3,1,2,0:T(8,128)(2,1)S(1)}, u32[]{:S(2)}, u32[]{:S(2)}) collective-permute-start(bf16[2,64,3,64]{3,1,2,0:T(8,128)(2,1)S(1)} %copy.201), channel_id=1, source_target_pairs={{30,0},{0,2},{2,4},{4,6},{6,8},{8,10},{10,12},{12,14},{14,16},{16,... | collective-permute-start | bytes 147464 | tf_op jit(solution)/shard_map/while/body/eval_jaxpr/ppermute | solution.py:17
  238.9 9.2 %collective-permute-start.3 = (bf16[2,64,3,64]{3,1,2,0:T(8,128)(2,1)S(1)}, bf16[2,64,3,64]{3,1,2,0:T(8,128)(2,1)S(1)}, u32[]{:S(2)}, u32[]{:S(2)}) collective-permute-start(bf16[2,64,3,64]{3,1,2,0:T(8,128)(2,1)S(1)} %fusion.155), channel_id=1, source_target_pairs={{30,0},{0,2},{2,4},{4,6},{6,8},{8,10},{10,12},{12,14},{14,16},{16,... | collective-permute-start | bytes 147464 | tf_op jit(solution)/shard_map/while/body/eval_jaxpr/ppermute | solution.py:17
  248.1 16.2 %collective-permute-start = (bf16[2,64,3,64]{3,1,2,0:T(8,128)(2,1)S(1)}, bf16[2,64,3,64]{3,1,2,0:T(8,128)(2,1)S(1)}, u32[]{:S(2)}, u32[]{:S(2)}) collective-permute-start(bf16[2,64,3,64]{3,1,2,0:T(8,128)(2,1)S(1)} %copy.200), channel_id=1, source_target_pairs={{30,0},{0,2},{2,4},{4,6},{6,8},{8,10},{10,12},{12,14},{14,16},{16,... | collective-permute-start | bytes 147464 | tf_op jit(solution)/shard_map/while/body/eval_jaxpr/ppermute | solution.py:17
  248.3 16.0 %collective-permute-start.1 = (bf16[2,64,3,64]{3,1,2,0:T(8,128)(2,1)S(1)}, bf16[2,64,3,64]{3,1,2,0:T(8,128)(2,1)S(1)}, u32[]{:S(2)}, u32[]{:S(2)}) collective-permute-start(bf16[2,64,3,64]{3,1,2,0:T(8,128)(2,1)S(1)} %copy.201), channel_id=1, source_target_pairs={{30,0},{0,2},{2,4},{4,6},{6,8},{8,10},{10,12},{12,14},{14,16},{16,... | collective-permute-start | bytes 147464 | tf_op jit(solution)/shard_map/while/body/eval_jaxpr/ppermute | solution.py:17
  264.3 14.5 %collective-permute-start = (bf16[2,64,3,64]{3,1,2,0:T(8,128)(2,1)S(1)}, bf16[2,64,3,64]{3,1,2,0:T(8,128)(2,1)S(1)}, u32[]{:S(2)}, u32[]{:S(2)}) collective-permute-start(bf16[2,64,3,64]{3,1,2,0:T(8,128)(2,1)S(1)} %copy.200), channel_id=1, source_target_pairs={{30,0},{0,2},{2,4},{4,6},{6,8},{8,10},{10,12},{12,14},{14,16},{16,... | collective-permute-start | bytes 147464 | tf_op jit(solution)/shard_map/while/body/eval_jaxpr/ppermute | solution.py:17
  264.4 14.4 %collective-permute-start.1 = (bf16[2,64,3,64]{3,1,2,0:T(8,128)(2,1)S(1)}, bf16[2,64,3,64]{3,1,2,0:T(8,128)(2,1)S(1)}, u32[]{:S(2)}, u32[]{:S(2)}) collective-permute-start(bf16[2,64,3,64]{3,1,2,0:T(8,128)(2,1)S(1)} %copy.201), channel_id=1, source_target_pairs={{30,0},{0,2},{2,4},{4,6},{6,8},{8,10},{10,12},{12,14},{14,16},{16,... | collective-permute-start | bytes 147464 | tf_op jit(solution)/shard_map/while/body/eval_jaxpr/ppermute | solution.py:17
  269.1 9.7 %collective-permute-start.3 = (bf16[2,64,3,64]{3,1,2,0:T(8,128)(2,1)S(1)}, bf16[2,64,3,64]{3,1,2,0:T(8,128)(2,1)S(1)}, u32[]{:S(2)}, u32[]{:S(2)}) collective-permute-start(bf16[2,64,3,64]{3,1,2,0:T(8,128)(2,1)S(1)} %fusion.155), channel_id=1, source_target_pairs={{30,0},{0,2},{2,4},{4,6},{6,8},{8,10},{10,12},{12,14},{14,16},{16,... | collective-permute-start | bytes 147464 | tf_op jit(solution)/shard_map/while/body/eval_jaxpr/ppermute | solution.py:17
  278.9 15.0 %collective-permute-start = (bf16[2,64,3,64]{3,1,2,0:T(8,128)(2,1)S(1)}, bf16[2,64,3,64]{3,1,2,0:T(8,128)(2,1)S(1)}, u32[]{:S(2)}, u32[]{:S(2)}) collective-permute-start(bf16[2,64,3,64]{3,1,2,0:T(8,128)(2,1)S(1)} %copy.200), channel_id=1, source_target_pairs={{30,0},{0,2},{2,4},{4,6},{6,8},{8,10},{10,12},{12,14},{14,16},{16,... | collective-permute-start | bytes 147464 | tf_op jit(solution)/shard_map/while/body/eval_jaxpr/ppermute | solution.py:17
  279.0 15.0 %collective-permute-start.1 = (bf16[2,64,3,64]{3,1,2,0:T(8,128)(2,1)S(1)}, bf16[2,64,3,64]{3,1,2,0:T(8,128)(2,1)S(1)}, u32[]{:S(2)}, u32[]{:S(2)}) collective-permute-start(bf16[2,64,3,64]{3,1,2,0:T(8,128)(2,1)S(1)} %copy.201), channel_id=1, source_target_pairs={{30,0},{0,2},{2,4},{4,6},{6,8},{8,10},{10,12},{12,14},{14,16},{16,... | collective-permute-start | bytes 147464 | tf_op jit(solution)/shard_map/while/body/eval_jaxpr/ppermute | solution.py:17
  282.7 9.3 %collective-permute-start.2 = (bf16[2,64,3,64]{3,1,2,0:T(8,128)(2,1)S(1)}, bf16[2,64,3,64]{3,1,2,0:T(8,128)(2,1)S(1)}, u32[]{:S(2)}, u32[]{:S(2)}) collective-permute-start(bf16[2,64,3,64]{3,1,2,0:T(8,128)(2,1)S(1)} %fusion.154), channel_id=1, source_target_pairs={{30,0},{0,2},{2,4},{4,6},{6,8},{8,10},{10,12},{12,14},{14,16},{16,... | collective-permute-start | bytes 147464 | tf_op jit(solution)/shard_map/while/body/eval_jaxpr/ppermute | solution.py:17
  283.1 10.8 %collective-permute-start.3 = (bf16[2,64,3,64]{3,1,2,0:T(8,128)(2,1)S(1)}, bf16[2,64,3,64]{3,1,2,0:T(8,128)(2,1)S(1)}, u32[]{:S(2)}, u32[]{:S(2)}) collective-permute-start(bf16[2,64,3,64]{3,1,2,0:T(8,128)(2,1)S(1)} %fusion.155), channel_id=1, source_target_pairs={{30,0},{0,2},{2,4},{4,6},{6,8},{8,10},{10,12},{12,14},{14,16},{16,... | collective-permute-start | bytes 147464 | tf_op jit(solution)/shard_map/while/body/eval_jaxpr/ppermute | solution.py:17
  294.0 15.4 %collective-permute-start = (bf16[2,64,3,64]{3,1,2,0:T(8,128)(2,1)S(1)}, bf16[2,64,3,64]{3,1,2,0:T(8,128)(2,1)S(1)}, u32[]{:S(2)}, u32[]{:S(2)}) collective-permute-start(bf16[2,64,3,64]{3,1,2,0:T(8,128)(2,1)S(1)} %copy.200), channel_id=1, source_target_pairs={{30,0},{0,2},{2,4},{4,6},{6,8},{8,10},{10,12},{12,14},{14,16},{16,... | collective-permute-start | bytes 147464 | tf_op jit(solution)/shard_map/while/body/eval_jaxpr/ppermute | solution.py:17
  294.1 15.4 %collective-permute-start.1 = (bf16[2,64,3,64]{3,1,2,0:T(8,128)(2,1)S(1)}, bf16[2,64,3,64]{3,1,2,0:T(8,128)(2,1)S(1)}, u32[]{:S(2)}, u32[]{:S(2)}) collective-permute-start(bf16[2,64,3,64]{3,1,2,0:T(8,128)(2,1)S(1)} %copy.201), channel_id=1, source_target_pairs={{30,0},{0,2},{2,4},{4,6},{6,8},{8,10},{10,12},{12,14},{14,16},{16,... | collective-permute-start | bytes 147464 | tf_op jit(solution)/shard_map/while/body/eval_jaxpr/ppermute | solution.py:17
  297.4 9.9 %collective-permute-start.2 = (bf16[2,64,3,64]{3,1,2,0:T(8,128)(2,1)S(1)}, bf16[2,64,3,64]{3,1,2,0:T(8,128)(2,1)S(1)}, u32[]{:S(2)}, u32[]{:S(2)}) collective-permute-start(bf16[2,64,3,64]{3,1,2,0:T(8,128)(2,1)S(1)} %fusion.154), channel_id=1, source_target_pairs={{30,0},{0,2},{2,4},{4,6},{6,8},{8,10},{10,12},{12,14},{14,16},{16,... | collective-permute-start | bytes 147464 | tf_op jit(solution)/shard_map/while/body/eval_jaxpr/ppermute | solution.py:17
  297.7 11.7 %collective-permute-start.3 = (bf16[2,64,3,64]{3,1,2,0:T(8,128)(2,1)S(1)}, bf16[2,64,3,64]{3,1,2,0:T(8,128)(2,1)S(1)}, u32[]{:S(2)}, u32[]{:S(2)}) collective-permute-start(bf16[2,64,3,64]{3,1,2,0:T(8,128)(2,1)S(1)} %fusion.155), channel_id=1, source_target_pairs={{30,0},{0,2},{2,4},{4,6},{6,8},{8,10},{10,12},{12,14},{14,16},{16,... | collective-permute-start | bytes 147464 | tf_op jit(solution)/shard_map/while/body/eval_jaxpr/ppermute | solution.py:17
  309.5 14.8 %collective-permute-start = (bf16[2,64,3,64]{3,1,2,0:T(8,128)(2,1)S(1)}, bf16[2,64,3,64]{3,1,2,0:T(8,128)(2,1)S(1)}, u32[]{:S(2)}, u32[]{:S(2)}) collective-permute-start(bf16[2,64,3,64]{3,1,2,0:T(8,128)(2,1)S(1)} %copy.200), channel_id=1, source_target_pairs={{30,0},{0,2},{2,4},{4,6},{6,8},{8,10},{10,12},{12,14},{14,16},{16,... | collective-permute-start | bytes 147464 | tf_op jit(solution)/shard_map/while/body/eval_jaxpr/ppermute | solution.py:17
  309.5 14.7 %collective-permute-start.1 = (bf16[2,64,3,64]{3,1,2,0:T(8,128)(2,1)S(1)}, bf16[2,64,3,64]{3,1,2,0:T(8,128)(2,1)S(1)}, u32[]{:S(2)}, u32[]{:S(2)}) collective-permute-start(bf16[2,64,3,64]{3,1,2,0:T(8,128)(2,1)S(1)} %copy.201), channel_id=1, source_target_pairs={{30,0},{0,2},{2,4},{4,6},{6,8},{8,10},{10,12},{12,14},{14,16},{16,... | collective-permute-start | bytes 147464 | tf_op jit(solution)/shard_map/while/body/eval_jaxpr/ppermute | solution.py:17
  312.9 10.0 %collective-permute-start.2 = (bf16[2,64,3,64]{3,1,2,0:T(8,128)(2,1)S(1)}, bf16[2,64,3,64]{3,1,2,0:T(8,128)(2,1)S(1)}, u32[]{:S(2)}, u32[]{:S(2)}) collective-permute-start(bf16[2,64,3,64]{3,1,2,0:T(8,128)(2,1)S(1)} %fusion.154), channel_id=1, source_target_pairs={{30,0},{0,2},{2,4},{4,6},{6,8},{8,10},{10,12},{12,14},{14,16},{16,... | collective-permute-start | bytes 147464 | tf_op jit(solution)/shard_map/while/body/eval_jaxpr/ppermute | solution.py:17
  313.2 11.0 %collective-permute-start.3 = (bf16[2,64,3,64]{3,1,2,0:T(8,128)(2,1)S(1)}, bf16[2,64,3,64]{3,1,2,0:T(8,128)(2,1)S(1)}, u32[]{:S(2)}, u32[]{:S(2)}) collective-permute-start(bf16[2,64,3,64]{3,1,2,0:T(8,128)(2,1)S(1)} %fusion.155), channel_id=1, source_target_pairs={{30,0},{0,2},{2,4},{4,6},{6,8},{8,10},{10,12},{12,14},{14,16},{16,... | collective-permute-start | bytes 147464 | tf_op jit(solution)/shard_map/while/body/eval_jaxpr/ppermute | solution.py:17
  324.3 14.1 %collective-permute-start = (bf16[2,64,3,64]{3,1,2,0:T(8,128)(2,1)S(1)}, bf16[2,64,3,64]{3,1,2,0:T(8,128)(2,1)S(1)}, u32[]{:S(2)}, u32[]{:S(2)}) collective-permute-start(bf16[2,64,3,64]{3,1,2,0:T(8,128)(2,1)S(1)} %copy.200), channel_id=1, source_target_pairs={{30,0},{0,2},{2,4},{4,6},{6,8},{8,10},{10,12},{12,14},{14,16},{16,... | collective-permute-start | bytes 147464 | tf_op jit(solution)/shard_map/while/body/eval_jaxpr/ppermute | solution.py:17
  324.4 14.0 %collective-permute-start.1 = (bf16[2,64,3,64]{3,1,2,0:T(8,128)(2,1)S(1)}, bf16[2,64,3,64]{3,1,2,0:T(8,128)(2,1)S(1)}, u32[]{:S(2)}, u32[]{:S(2)}) collective-permute-start(bf16[2,64,3,64]{3,1,2,0:T(8,128)(2,1)S(1)} %copy.201), channel_id=1, source_target_pairs={{30,0},{0,2},{2,4},{4,6},{6,8},{8,10},{10,12},{12,14},{14,16},{16,... | collective-permute-start | bytes 147464 | tf_op jit(solution)/shard_map/while/body/eval_jaxpr/ppermute | solution.py:17
  327.7 9.4 %collective-permute-start.2 = (bf16[2,64,3,64]{3,1,2,0:T(8,128)(2,1)S(1)}, bf16[2,64,3,64]{3,1,2,0:T(8,128)(2,1)S(1)}, u32[]{:S(2)}, u32[]{:S(2)}) collective-permute-start(bf16[2,64,3,64]{3,1,2,0:T(8,128)(2,1)S(1)} %fusion.154), channel_id=1, source_target_pairs={{30,0},{0,2},{2,4},{4,6},{6,8},{8,10},{10,12},{12,14},{14,16},{16,... | collective-permute-start | bytes 147464 | tf_op jit(solution)/shard_map/while/body/eval_jaxpr/ppermute | solution.py:17
  328.1 10.3 %collective-permute-start.3 = (bf16[2,64,3,64]{3,1,2,0:T(8,128)(2,1)S(1)}, bf16[2,64,3,64]{3,1,2,0:T(8,128)(2,1)S(1)}, u32[]{:S(2)}, u32[]{:S(2)}) collective-permute-start(bf16[2,64,3,64]{3,1,2,0:T(8,128)(2,1)S(1)} %fusion.155), channel_id=1, source_target_pairs={{30,0},{0,2},{2,4},{4,6},{6,8},{8,10},{10,12},{12,14},{14,16},{16,... | collective-permute-start | bytes 147464 | tf_op jit(solution)/shard_map/while/body/eval_jaxpr/ppermute | solution.py:17
  338.4 13.9 %collective-permute-start = (bf16[2,64,3,64]{3,1,2,0:T(8,128)(2,1)S(1)}, bf16[2,64,3,64]{3,1,2,0:T(8,128)(2,1)S(1)}, u32[]{:S(2)}, u32[]{:S(2)}) collective-permute-start(bf16[2,64,3,64]{3,1,2,0:T(8,128)(2,1)S(1)} %copy.200), channel_id=1, source_target_pairs={{30,0},{0,2},{2,4},{4,6},{6,8},{8,10},{10,12},{12,14},{14,16},{16,... | collective-permute-start | bytes 147464 | tf_op jit(solution)/shard_map/while/body/eval_jaxpr/ppermute | solution.py:17
  338.5 13.9 %collective-permute-start.1 = (bf16[2,64,3,64]{3,1,2,0:T(8,128)(2,1)S(1)}, bf16[2,64,3,64]{3,1,2,0:T(8,128)(2,1)S(1)}, u32[]{:S(2)}, u32[]{:S(2)}) collective-permute-start(bf16[2,64,3,64]{3,1,2,0:T(8,128)(2,1)S(1)} %copy.201), channel_id=1, source_target_pairs={{30,0},{0,2},{2,4},{4,6},{6,8},{8,10},{10,12},{12,14},{14,16},{16,... | collective-permute-start | bytes 147464 | tf_op jit(solution)/shard_map/while/body/eval_jaxpr/ppermute | solution.py:17
  341.8 9.4 %collective-permute-start.2 = (bf16[2,64,3,64]{3,1,2,0:T(8,128)(2,1)S(1)}, bf16[2,64,3,64]{3,1,2,0:T(8,128)(2,1)S(1)}, u32[]{:S(2)}, u32[]{:S(2)}) collective-permute-start(bf16[2,64,3,64]{3,1,2,0:T(8,128)(2,1)S(1)} %fusion.154), channel_id=1, source_target_pairs={{30,0},{0,2},{2,4},{4,6},{6,8},{8,10},{10,12},{12,14},{14,16},{16,... | collective-permute-start | bytes 147464 | tf_op jit(solution)/shard_map/while/body/eval_jaxpr/ppermute | solution.py:17
  342.2 10.2 %collective-permute-start.3 = (bf16[2,64,3,64]{3,1,2,0:T(8,128)(2,1)S(1)}, bf16[2,64,3,64]{3,1,2,0:T(8,128)(2,1)S(1)}, u32[]{:S(2)}, u32[]{:S(2)}) collective-permute-start(bf16[2,64,3,64]{3,1,2,0:T(8,128)(2,1)S(1)} %fusion.155), channel_id=1, source_target_pairs={{30,0},{0,2},{2,4},{4,6},{6,8},{8,10},{10,12},{12,14},{14,16},{16,... | collective-permute-start | bytes 147464 | tf_op jit(solution)/shard_map/while/body/eval_jaxpr/ppermute | solution.py:17
  352.4 13.8 %collective-permute-start = (bf16[2,64,3,64]{3,1,2,0:T(8,128)(2,1)S(1)}, bf16[2,64,3,64]{3,1,2,0:T(8,128)(2,1)S(1)}, u32[]{:S(2)}, u32[]{:S(2)}) collective-permute-start(bf16[2,64,3,64]{3,1,2,0:T(8,128)(2,1)S(1)} %copy.200), channel_id=1, source_target_pairs={{30,0},{0,2},{2,4},{4,6},{6,8},{8,10},{10,12},{12,14},{14,16},{16,... | collective-permute-start | bytes 147464 | tf_op jit(solution)/shard_map/while/body/eval_jaxpr/ppermute | solution.py:17
  352.5 13.8 %collective-permute-start.1 = (bf16[2,64,3,64]{3,1,2,0:T(8,128)(2,1)S(1)}, bf16[2,64,3,64]{3,1,2,0:T(8,128)(2,1)S(1)}, u32[]{:S(2)}, u32[]{:S(2)}) collective-permute-start(bf16[2,64,3,64]{3,1,2,0:T(8,128)(2,1)S(1)} %copy.201), channel_id=1, source_target_pairs={{30,0},{0,2},{2,4},{4,6},{6,8},{8,10},{10,12},{12,14},{14,16},{16,... | collective-permute-start | bytes 147464 | tf_op jit(solution)/shard_map/while/body/eval_jaxpr/ppermute | solution.py:17
  355.8 9.4 %collective-permute-start.2 = (bf16[2,64,3,64]{3,1,2,0:T(8,128)(2,1)S(1)}, bf16[2,64,3,64]{3,1,2,0:T(8,128)(2,1)S(1)}, u32[]{:S(2)}, u32[]{:S(2)}) collective-permute-start(bf16[2,64,3,64]{3,1,2,0:T(8,128)(2,1)S(1)} %fusion.154), channel_id=1, source_target_pairs={{30,0},{0,2},{2,4},{4,6},{6,8},{8,10},{10,12},{12,14},{14,16},{16,... | collective-permute-start | bytes 147464 | tf_op jit(solution)/shard_map/while/body/eval_jaxpr/ppermute | solution.py:17
  356.2 10.1 %collective-permute-start.3 = (bf16[2,64,3,64]{3,1,2,0:T(8,128)(2,1)S(1)}, bf16[2,64,3,64]{3,1,2,0:T(8,128)(2,1)S(1)}, u32[]{:S(2)}, u32[]{:S(2)}) collective-permute-start(bf16[2,64,3,64]{3,1,2,0:T(8,128)(2,1)S(1)} %fusion.155), channel_id=1, source_target_pairs={{30,0},{0,2},{2,4},{4,6},{6,8},{8,10},{10,12},{12,14},{14,16},{16,... | collective-permute-start | bytes 147464 | tf_op jit(solution)/shard_map/while/body/eval_jaxpr/ppermute | solution.py:17
  366.3 13.0 %collective-permute-start = (bf16[2,64,3,64]{3,1,2,0:T(8,128)(2,1)S(1)}, bf16[2,64,3,64]{3,1,2,0:T(8,128)(2,1)S(1)}, u32[]{:S(2)}, u32[]{:S(2)}) collective-permute-start(bf16[2,64,3,64]{3,1,2,0:T(8,128)(2,1)S(1)} %copy.200), channel_id=1, source_target_pairs={{30,0},{0,2},{2,4},{4,6},{6,8},{8,10},{10,12},{12,14},{14,16},{16,... | collective-permute-start | bytes 147464 | tf_op jit(solution)/shard_map/while/body/eval_jaxpr/ppermute | solution.py:17
  366.4 13.0 %collective-permute-start.1 = (bf16[2,64,3,64]{3,1,2,0:T(8,128)(2,1)S(1)}, bf16[2,64,3,64]{3,1,2,0:T(8,128)(2,1)S(1)}, u32[]{:S(2)}, u32[]{:S(2)}) collective-permute-start(bf16[2,64,3,64]{3,1,2,0:T(8,128)(2,1)S(1)} %copy.201), channel_id=1, source_target_pairs={{30,0},{0,2},{2,4},{4,6},{6,8},{8,10},{10,12},{12,14},{14,16},{16,... | collective-permute-start | bytes 147464 | tf_op jit(solution)/shard_map/while/body/eval_jaxpr/ppermute | solution.py:17
  370.4 9.0 %collective-permute-start.3 = (bf16[2,64,3,64]{3,1,2,0:T(8,128)(2,1)S(1)}, bf16[2,64,3,64]{3,1,2,0:T(8,128)(2,1)S(1)}, u32[]{:S(2)}, u32[]{:S(2)}) collective-permute-start(bf16[2,64,3,64]{3,1,2,0:T(8,128)(2,1)S(1)} %fusion.155), channel_id=1, source_target_pairs={{30,0},{0,2},{2,4},{4,6},{6,8},{8,10},{10,12},{12,14},{14,16},{16,... | collective-permute-start | bytes 147464 | tf_op jit(solution)/shard_map/while/body/eval_jaxpr/ppermute | solution.py:17
  390.3 15.0 %reduce-scatter.10.cloned.1.call-start = ((), (), s32[]{:S(2)}) async-start(), calls=%async_computation.11 | async-start | bytes 442368 | tf_op jit(solution)/shard_map/reduce_scatter | solution.py:314
  391.7 25.1 %reduce-scatter.14.cloned.1.call-start = ((), (), s32[]{:S(2)}) async-start(), calls=%async_computation.13 | async-start | bytes 1105920 | tf_op jit(solution)/shard_map/reduce_scatter | solution.py:320
  393.0 36.0 %reduce-scatter.8.cloned.1.call-start = ((), (), s32[]{:S(2)}) async-start(), calls=%async_computation.10 | async-start | bytes 1105920 | tf_op jit(solution)/shard_map/reduce_scatter | solution.py:311
  395.5 46.8 %reduce-scatter.18.cloned.1.call-start = ((), (), s32[]{:S(2)}) async-start(), calls=%async_computation.15 | async-start | bytes 2654208 | tf_op jit(solution)/shard_map/reduce_scatter | solution.py:329
  397.5 58.3 %reduce-scatter.16.cloned.1.call-start = ((), (), s32[]{:S(2)}) async-start(), calls=%async_computation.14 | async-start | bytes 2654208 | tf_op jit(solution)/shard_map/reduce_scatter | solution.py:326
  399.4 69.6 %reduce-scatter.20.cloned.1.call-start = ((), (), s32[]{:S(2)}) async-start(), calls=%async_computation.16 | async-start | bytes 2654208 | tf_op jit(solution)/shard_map/reduce_scatter | solution.py:332
  401.3 238.7 %all-reduce.10.cloned.1.call-start = ((), (), s32[]{:S(2)}) async-start(), calls=%async_computation.17 | async-start | bytes 7372800 | tf_op jit(solution)/shard_map/psum | solution.py:340
  (60 other events, 643.9 us)
Sparse Core Ops, SparseCore 0:
  9.6 12.7 all-gather.3
  24.0 11.2 all-gather.5
  36.8 11.2 all-gather.7
  390.5 3.8 reduce-scatter.11
  396.4 8.8 reduce-scatter.9
  407.4 9.3 reduce-scatter.13
  419.6 9.3 reduce-scatter.7
  431.9 10.4 reduce-scatter.17
  445.3 10.4 reduce-scatter.15
  458.5 10.4 reduce-scatter.19
  476.6 163.4 all-reduce.9
where the time goes:
time: 657 us; the launch traced here: 655 us
  waiting for transfers between devices  310 us (47%)
  blocking collectives  162 us (25%)
  matrix products  68.4 us (10%)
  other arithmetic  44.1 us (7%)
  starting transfers between devices  41.7 us (6%)
  between operations  16.2 us (2%)
  local copies, waits for them, and re-layouts  10.6 us (2%)
    ppermute x62, waiting for transfers between devices, shifted(): return lax.ppermute(block, axis, route)  123 us
    psum x1, waiting for transfers between devices, local(): lax.psum(owned_grads[0].astype(jnp.bfloat16), 'ctx').astype(jnp.float32)  118 us
    all_gather x1, blocking collectives, local(): key_part = lax.all_gather(key_rows, 'ctx', axis=1, tiled=True)  54.9 us
    all_gather x1, blocking collectives, local(): value_part = lax.all_gather(value_rows, 'ctx', axis=1, tiled=True)  49.6 us
    psum x1, blocking collectives, local(): lax.psum(owned_grads[4].astype(jnp.bfloat16), 'ctx').astype(jnp.float32)  43.7 us
    ppermute x62, starting transfers between devices, shifted(): return lax.ppermute(block, axis, route)  41 us
    dot_general x16, matrix products, block_grads(): jnp.einsum('sqkgd,snkd->skgqn', queries, key_part, preferred_element_type...  17 us
    reduce_scatter x1, waiting for transfers between devices, local(): lax.psum_scatter(grad_wgate.astype(jnp.bfloat16), 'fsdp', scatter_dimensi...  13.4 us
  transfers between devices with their start and end apart: 73, of which 38 were waited for; matrix products, arithmetic and copies ran while one was open for 16% of the time, Pallas kernels for 0%

commit v1 on v0

--- a/solution.py
+++ b/solution.py
@@ -9,6 +9,18 @@
 epsilon = 1e-05
 theta_base = 100000.0
 masked_value = -1e30
+
+
+def collect(x, axis, dim):
+    ways, here = (lax.axis_size(axis), lax.axis_index(axis))
+    grown, reach = (x, 1)
+    while reach < ways:
+        theirs = lax.ppermute(grown, axis, [(d, d ^ reach) for d in range(ways)])
+        mine_first = jnp.concatenate([grown, theirs], axis=dim)
+        theirs_first = jnp.concatenate([theirs, grown], axis=dim)
+        grown = jnp.where(here & reach == 0, mine_first, theirs_first)
+        reach = 2 * reach
+    return grown
 
 
 def shifted(block, axis, distance):
@@ -146,7 +158,7 @@
     )
     stat_shape = (seq_count, KV_HEADS, group_size, tok_count)
     running_max = jnp.full(stat_shape, masked_value, jnp.float32)
-    key_part = lax.all_gather(key_rows, "ctx", axis=1, tiled=True)
+    key_part = collect(key_rows, "ctx", 1)
     value_part = lax.all_gather(value_rows, "ctx", axis=1, tiled=True)
     key_pos = slot_positions(block_of_slot, jnp.int32(0), key_part.shape[1], half_len)
     visible = query_pos[:, None] >= key_pos[None, :]

time: 657 us -> 616 us (0.938)
  blocking collectives: 162 us -> 109 us
  starting transfers between devices: 41.7 us -> 62.7 us
  waiting for transfers between devices: 310 us -> 324 us
  other arithmetic: 44.1 us -> 31.9 us
  matrix products: 68.4 us -> 57 us
    all_gather x1 -> x0, blocking collectives: 54.9 us -> none  [local(): key_part = lax.all_gather(key_rows, 'ctx', axis=1, tiled=True)]
    convert_element_type x15, other arithmetic: 0.22 us -> 13.6 us  [one_hop(): shifted((grad_value + grad_value_part).astype(jnp.bfloat16), 'ctx', 1)]
    ppermute x62, starting transfers between devices: 41 us -> 53.3 us  [shifted(): return lax.ppermute(block, axis, route)]
    dot_general x16, matrix products: 17 us -> 5.74 us  [block_grads(): jnp.einsum('sqkgd,snkd->skgqn', queries, key_part, preferred_element_type...]
    reduce_sum x17, other arithmetic: 12.7 us -> 1.53 us  [slot_positions(): owners = jnp.sum(jnp.where(slot_match, block_of_slot[None, :], 0), axis=1)]
    ppermute x62, waiting for transfers between devices: 123 us -> 133 us  [shifted(): return lax.ppermute(block, axis, route)]
    ge x16, other arithmetic: 12.3 us -> 1.83 us  [block_grads(): visible = query_pos[:, None] >= key_pos[None, :]]
    ppermute x0 -> x4, starting transfers between devices: none -> 8.73 us  [collect(): theirs = lax.ppermute(grown, axis, [(d, d ^ reach) for d in range(ways)])]
  transfers between devices with their start and end apart: 73 -> 77, of which waited for: 38 -> 40; matrix products, arithmetic and copies ran while one was open for 16% -> 13% of each run, Pallas kernels for 0% -> 0%
where the time goes in v1:
time: 616 us; the launch traced here: 615 us
  waiting for transfers between devices  324 us (53%)
  blocking collectives  109 us (18%)
  starting transfers between devices  62.7 us (10%)
  matrix products  57 us (9%)
  other arithmetic  31.9 us (5%)
  between operations  16.4 us (3%)
  local copies, waits for them, and re-layouts  10.9 us (2%)
    ppermute x62, waiting for transfers between devices, shifted(): return lax.ppermute(block, axis, route)  133 us
    psum x1, waiting for transfers between devices, local(): lax.psum(owned_grads[0].astype(jnp.bfloat16), 'ctx').astype(jnp.float32)  118 us
    ppermute x62, starting transfers between devices, shifted(): return lax.ppermute(block, axis, route)  53.3 us
    all_gather x1, blocking collectives, local(): value_part = lax.all_gather(value_rows, 'ctx', axis=1, tiled=True)  51.4 us
    psum x1, blocking collectives, local(): lax.psum(owned_grads[4].astype(jnp.bfloat16), 'ctx').astype(jnp.float32)  43.7 us
    convert_element_type x15, other arithmetic, one_hop(): shifted((grad_value + grad_value_part).astype(jnp.bfloat16), 'ctx', 1)  13.6 us
    reduce_scatter x1, waiting for transfers between devices, local(): lax.psum_scatter(grad_wgate.astype(jnp.bfloat16), 'fsdp', scatter_dimensi...  13.4 us
    reduce_scatter x1, waiting for transfers between devices, local(): lax.psum_scatter(grad_wup.astype(jnp.bfloat16), 'fsdp', scatter_dimension...  13.3 us
  transfers between devices with their start and end apart: 77, of which 40 were waited for; matrix products, arithmetic and copies ran while one was open for 13% of the time, Pallas kernels for 0%

profile of v1, /device:TPU:0, one launch (start us, length us, event | category | flops | bytes accessed | tf_op | source)
XLA Modules:
  0.0 614.8 jit_solution(11398062615757228413)
XLA Ops:
  10.6 2.6 all-reduce.7
  13.2 2.1 all_gather.31
  16.7 2.9 collective-permute-start.4
  19.7 2.8 all_gather.32
  23.8 2.0 all_gather.33
  28.6 2.3 all_gather.35
  34.3 3.9 collective-permute-done.6
  38.3 2.6 collective-permute-start.7
  43.0 51.4 %all_gather.34 = bf16[2,1024,3,64]{3,0,2,1:T(2,128)(2,1)S(1)} all-gather(bf16[2,64,3,64]{3,0,2,1:T(2,128)(2,1)S(1)} %copy.115), channel_id=1, replica_groups=mesh['ctx'=16,'fsdp'=2] {'ctx'}, dimensions={1}, use_global_device_ids=true | all-gather | bytes 835584 | tf_op jit(solution)/shard_map/all_gather | solution.py:162
  94.4 2.1 fusion.17
  98.0 2.5 fusion.48
  101.7 2.9 fusion.82
  104.6 2.9 fusion.83
  107.5 3.5 multiply_convert_fusion
  116.3 221.8 %while.25 = (s32[]{:T(128)}, bf16[2,64,3,64]{3,1,2,0:T(8,128)(2,1)S(1)}, bf16[2,64,3,64]{3,1,2,0:T(8,128)(2,1)S(1)}, f32[2,3,3,64,64]{4,3,2,1,0:T(8,128)S(1)}, f...) while((s32[]{:T(128)}, ...), condition=%wide.region_10.11_spmd.clone, body=%wide.region_8.10_spmd.clone.sunk | while | flops 48082768 | bytes 4246918 | solution.py:269
  116.3 3.6 collective-permute-start
  119.9 3.4 collective-permute-start.1
  126.0 4.3 collective-permute-start.3
  130.6 3.1 collective-permute-done.2
  136.6 2.1 collective-permute-start.1
  140.6 3.1 collective-permute-start.3
  144.0 4.1 collective-permute-done.2
  148.1 2.2 collective-permute-done.3
  153.8 3.1 collective-permute-start.3
  157.3 5.4 collective-permute-done.2
  162.8 2.2 collective-permute-done.3
  167.9 3.6 collective-permute-start.3
  171.9 6.6 %collective-permute-done.2 = bf16[2,64,3,64]{3,1,2,0:T(8,128)(2,1)S(1)} collective-permute-done((bf16[2,64,3,64]{3,1,2,0:T(8,128)(2,1)S(1)}, bf16[2,64,3,64]{3,1,2,0:T(8,128)(2,1)S(1)}, u32[]{:S(2)}, u32[]{:S(2)}) %collective-permute-start.2) | collective-permute-done | bytes 49184 | tf_op jit(solution)/shard_map/while/body/eval_jaxpr/ppermute | solution.py:29
  178.5 2.2 collective-permute-done.3
  183.4 2.2 collective-permute-start.3
  186.0 9.2 %collective-permute-done.2 = bf16[2,64,3,64]{3,1,2,0:T(8,128)(2,1)S(1)} collective-permute-done((bf16[2,64,3,64]{3,1,2,0:T(8,128)(2,1)S(1)}, bf16[2,64,3,64]{3,1,2,0:T(8,128)(2,1)S(1)}, u32[]{:S(2)}, u32[]{:S(2)}) %collective-permute-start.2) | collective-permute-done | bytes 49184 | tf_op jit(solution)/shard_map/while/body/eval_jaxpr/ppermute | solution.py:29
  195.2 2.0 collective-permute-done.3
  200.3 11.3 %collective-permute-done.2 = bf16[2,64,3,64]{3,1,2,0:T(8,128)(2,1)S(1)} collective-permute-done((bf16[2,64,3,64]{3,1,2,0:T(8,128)(2,1)S(1)}, bf16[2,64,3,64]{3,1,2,0:T(8,128)(2,1)S(1)}, u32[]{:S(2)}, u32[]{:S(2)}) %collective-permute-start.2) | collective-permute-done | bytes 49184 | tf_op jit(solution)/shard_map/while/body/eval_jaxpr/ppermute | solution.py:29
  216.0 10.4 %collective-permute-done.2 = bf16[2,64,3,64]{3,1,2,0:T(8,128)(2,1)S(1)} collective-permute-done((bf16[2,64,3,64]{3,1,2,0:T(8,128)(2,1)S(1)}, bf16[2,64,3,64]{3,1,2,0:T(8,128)(2,1)S(1)}, u32[]{:S(2)}, u32[]{:S(2)}) %collective-permute-start.2) | collective-permute-done | bytes 49184 | tf_op jit(solution)/shard_map/while/body/eval_jaxpr/ppermute | solution.py:29
  230.6 9.3 %collective-permute-done.2 = bf16[2,64,3,64]{3,1,2,0:T(8,128)(2,1)S(1)} collective-permute-done((bf16[2,64,3,64]{3,1,2,0:T(8,128)(2,1)S(1)}, bf16[2,64,3,64]{3,1,2,0:T(8,128)(2,1)S(1)}, u32[]{:S(2)}, u32[]{:S(2)}) %collective-permute-start.2) | collective-permute-done | bytes 49184 | tf_op jit(solution)/shard_map/while/body/eval_jaxpr/ppermute | solution.py:29
  244.3 8.3 %collective-permute-done.2 = bf16[2,64,3,64]{3,1,2,0:T(8,128)(2,1)S(1)} collective-permute-done((bf16[2,64,3,64]{3,1,2,0:T(8,128)(2,1)S(1)}, bf16[2,64,3,64]{3,1,2,0:T(8,128)(2,1)S(1)}, u32[]{:S(2)}, u32[]{:S(2)}) %collective-permute-start.2) | collective-permute-done | bytes 49184 | tf_op jit(solution)/shard_map/while/body/eval_jaxpr/ppermute | solution.py:29
  256.9 8.2 %collective-permute-done.2 = bf16[2,64,3,64]{3,1,2,0:T(8,128)(2,1)S(1)} collective-permute-done((bf16[2,64,3,64]{3,1,2,0:T(8,128)(2,1)S(1)}, bf16[2,64,3,64]{3,1,2,0:T(8,128)(2,1)S(1)}, u32[]{:S(2)}, u32[]{:S(2)}) %collective-permute-start.2) | collective-permute-done | bytes 49184 | tf_op jit(solution)/shard_map/while/body/eval_jaxpr/ppermute | solution.py:29
  268.9 2.9 collective-permute-start.3
  272.1 5.4 collective-permute-done.2
  281.1 2.6 collective-permute-start.2
  284.0 3.1 collective-permute-start.3
  287.4 2.6 collective-permute-done.2
  290.1 3.2 collective-permute-done.3
  294.4 2.9 collective-permute-start.1
  299.2 3.7 collective-permute-start.3
  303.2 4.6 collective-permute-done.2
  307.8 2.2 collective-permute-done.3
  312.8 4.1 collective-permute-start.3
  317.3 6.2 %collective-permute-done.2 = bf16[2,64,3,64]{3,1,2,0:T(8,128)(2,1)S(1)} collective-permute-done((bf16[2,64,3,64]{3,1,2,0:T(8,128)(2,1)S(1)}, bf16[2,64,3,64]{3,1,2,0:T(8,128)(2,1)S(1)}, u32[]{:S(2)}, u32[]{:S(2)}) %collective-permute-start.2) | collective-permute-done | bytes 49184 | tf_op jit(solution)/shard_map/while/body/eval_jaxpr/ppermute | solution.py:29
  327.3 2.3 collective-permute-start.3
  330.0 6.0 collective-permute-done.2
  340.2 7.8 %collective-permute-done.9 = bf16[2,64,3,64]{1,3,2,0:T(8,128)(2,1)} collective-permute-done((bf16[2,64,3,64]{1,3,2,0:T(8,128)(2,1)}, bf16[2,64,3,64]{1,3,2,0:T(8,128)(2,1)}, u32[]{:S(2)}, u32[]{:S(2)}) %collective-permute-start.9) | collective-permute-done | bytes 49184 | tf_op jit(solution)/shard_map/ppermute | solution.py:29
  359.5 1.9 convolution_convert_fusion
  361.5 3.3 reduce-scatter.10.cloned.1.call-done
  364.8 11.5 %reduce-scatter.14.cloned.1.call-done = bf16[288,576]{1,0:T(8,128)(2,1)} async-done(((bf16[576,576]{1,0:T(8,128)(2,1)}), bf16[288,576]{1,0:T(8,128)(2,1)}) %reduce-scatter.14.cloned.1.call-update) | async-done | bytes 331792 | tf_op jit(solution)/shard_map/reduce_scatter | solution.py:332
  376.3 12.2 %reduce-scatter.8.cloned.1.call-done = bf16[288,576]{1,0:T(8,128)(2,1)} async-done(((bf16[576,576]{1,0:T(8,128)(2,1)}), bf16[288,576]{1,0:T(8,128)(2,1)}) %reduce-scatter.8.cloned.1.call-update) | async-done | bytes 331792 | tf_op jit(solution)/shard_map/reduce_scatter | solution.py:323
  388.5 13.3 %reduce-scatter.18.cloned.1.call-done = bf16[288,1536]{1,0:T(8,128)(2,1)} async-done(((bf16[576,1536]{1,0:T(8,128)(2,1)}), bf16[288,1536]{1,0:T(8,128)(2,1)}) %reduce-scatter.18.cloned.1.call-update) | async-done | bytes 884752 | tf_op jit(solution)/shard_map/reduce_scatter | solution.py:341
  401.8 13.4 %reduce-scatter.16.cloned.1.call-done = bf16[288,1536]{1,0:T(8,128)(2,1)} async-done(((bf16[576,1536]{1,0:T(8,128)(2,1)}), bf16[288,1536]{1,0:T(8,128)(2,1)}) %reduce-scatter.16.cloned.1.call-update) | async-done | bytes 884752 | tf_op jit(solution)/shard_map/reduce_scatter | solution.py:338
  415.3 13.2 %reduce-scatter.20.cloned.1.call-done = bf16[768,576]{0,1:T(8,128)(2,1)} async-done(((bf16[1536,576]{0,1:T(8,128)(2,1)}), bf16[768,576]{0,1:T(8,128)(2,1)}) %reduce-scatter.20.cloned.1.call-update) | async-done | bytes 884752 | tf_op jit(solution)/shard_map/reduce_scatter | solution.py:344
  429.2 2.1 fusion.31
  433.2 2.5 all-reduce.6
  435.9 43.7 %all-reduce.4 = (bf16[288]{0:T(512)(128)(2,1)S(1)}, bf16[288]{0:T(512)(128)(2,1)S(1)}) all-reduce(bf16[288]{0:T(512)(128)(2,1)S(1)} %dynamic-slice.3, bf16[288]{0:T(512)(128)(2,1)S(1)} %dynamic-slice.5), channel_id=1, replica_groups=mesh['ctx'=16,'fsdp'=2] {'ctx'}, use_global_device_ids=true, to_apply=%region_23.24 | all-reduce | flops 576 | bytes 2304 | tf_op jit(solution)/shard_map/psum | solution.py:356
  481.7 117.8 %all-reduce.10.cloned.1.call-done = (bf16[288,576]{1,0:T(8,128)(2,1)}, bf16[288,192]{1,0:T(8,128)(2,1)}, bf16[288,192]{1,0:T(8,128)(2,1)}, bf16[288,576]{1,0:T(8...) async-done(((bf16[288,576]{1,0:T(8,128)(2,1)}, bf16[288,192]{1,0:T(8,128)(2,1)}, bf16[288,192]{1,0:T(8,128)(2,1)}, ...) | async-done | bytes 3538960 | tf_op jit(solution)/shard_map/psum | solution.py:352
  599.5 2.7 convert_element_type.301
  (536 shorter events, 102.7 us)
Async XLA Ops:
  7.2 94.4 %all-gather.4.cloned.1.call-start = ((), (), s32[]{:S(2)}) async-start(), calls=%async_computation.7 | async-start | bytes 2654208 | tf_op jit(solution)/shard_map/all_gather | solution.py:112
  8.0 96.6 %all-gather.6.cloned.1.call-start = ((), (), s32[]{:S(2)}) async-start(), calls=%async_computation.8 | async-start | bytes 2654208 | tf_op jit(solution)/shard_map/all_gather | solution.py:113
  8.7 98.7 %all-gather.8.cloned.1.call-start = ((), (), s32[]{:S(2)}) async-start(), calls=%async_computation.9 | async-start | bytes 2654208 | tf_op jit(solution)/shard_map/all_gather | solution.py:114
  16.7 10.2 %collective-permute-start.4 = (bf16[2,64,3,64]{1,3,2,0:T(8,128)(2,1)S(1)}, bf16[2,64,3,64]{1,3,2,0:T(8,128)(2,1)S(1)}, u32[]{:S(2)}, u32[]{:S(2)}) collective-permute-start(bf16[2,64,3,64]{1,3,2,0:T(8,128)(2,1)S(1)} %pad_maximum_fusion.1), channel_id=1, source_target_pairs={{0,2},{2,0},{4,6},{6,4},{8,10},{10,8},{12,14},{14,12},{16,18},{18,... | collective-permute-start | bytes 147464 | tf_op jit(solution)/shard_map/ppermute | solution.py:18
  19.6 341.9 %reduce-scatter.12.cloned.1.call-start = ((), (), s32[]{:S(2)}) async-start(), calls=%async_computation.12 | async-start | bytes 442368 | tf_op jit(solution)/shard_map/reduce_scatter | solution.py:329
  38.3 56.1 %collective-permute-start.7 = (bf16[2,512,3,64]{1,3,2,0:T(8,128)(2,1)S(1)}, bf16[2,512,3,64]{1,3,2,0:T(8,128)(2,1)}, u32[]{:S(2)}, u32[]{:S(2)}) collective-permute-start(bf16[2,512,3,64]{1,3,2,0:T(8,128)(2,1)S(1)} %maximum_select_fusion.1), channel_id=1, source_target_pairs={{0,16},{2,18},{4,20},{6,22},{8,24},{10,26},{12,28},{14,30},{16,0},... | collective-permute-start | bytes 1179656 | tf_op jit(solution)/shard_map/ppermute | solution.py:18
  116.3 19.6 %collective-permute-start = (bf16[2,64,3,64]{3,1,2,0:T(8,128)(2,1)S(1)}, bf16[2,64,3,64]{3,1,2,0:T(8,128)(2,1)S(1)}, u32[]{:S(2)}, u32[]{:S(2)}) collective-permute-start(bf16[2,64,3,64]{3,1,2,0:T(8,128)(2,1)S(1)} %copy.188), channel_id=1, source_target_pairs={{30,0},{0,2},{2,4},{4,6},{6,8},{8,10},{10,12},{12,14},{14,16},{16,... | collective-permute-start | bytes 147464 | tf_op jit(solution)/shard_map/while/body/eval_jaxpr/ppermute | solution.py:29
  119.9 16.0 %collective-permute-start.1 = (bf16[2,64,3,64]{3,1,2,0:T(8,128)(2,1)S(1)}, bf16[2,64,3,64]{3,1,2,0:T(8,128)(2,1)S(1)}, u32[]{:S(2)}, u32[]{:S(2)}) collective-permute-start(bf16[2,64,3,64]{3,1,2,0:T(8,128)(2,1)S(1)} %copy.189), channel_id=1, source_target_pairs={{30,0},{0,2},{2,4},{4,6},{6,8},{8,10},{10,12},{12,14},{14,16},{16,... | collective-permute-start | bytes 147464 | tf_op jit(solution)/shard_map/while/body/eval_jaxpr/ppermute | solution.py:29
  136.0 15.3 %collective-permute-start = (bf16[2,64,3,64]{3,1,2,0:T(8,128)(2,1)S(1)}, bf16[2,64,3,64]{3,1,2,0:T(8,128)(2,1)S(1)}, u32[]{:S(2)}, u32[]{:S(2)}) collective-permute-start(bf16[2,64,3,64]{3,1,2,0:T(8,128)(2,1)S(1)} %copy.188), channel_id=1, source_target_pairs={{30,0},{0,2},{2,4},{4,6},{6,8},{8,10},{10,12},{12,14},{14,16},{16,... | collective-permute-start | bytes 147464 | tf_op jit(solution)/shard_map/while/body/eval_jaxpr/ppermute | solution.py:29
  136.6 14.7 %collective-permute-start.1 = (bf16[2,64,3,64]{3,1,2,0:T(8,128)(2,1)S(1)}, bf16[2,64,3,64]{3,1,2,0:T(8,128)(2,1)S(1)}, u32[]{:S(2)}, u32[]{:S(2)}) collective-permute-start(bf16[2,64,3,64]{3,1,2,0:T(8,128)(2,1)S(1)} %copy.189), channel_id=1, source_target_pairs={{30,0},{0,2},{2,4},{4,6},{6,8},{8,10},{10,12},{12,14},{14,16},{16,... | collective-permute-start | bytes 147464 | tf_op jit(solution)/shard_map/while/body/eval_jaxpr/ppermute | solution.py:29
  140.6 9.8 %collective-permute-start.3 = (bf16[2,64,3,64]{3,1,2,0:T(8,128)(2,1)S(1)}, bf16[2,64,3,64]{3,1,2,0:T(8,128)(2,1)}, u32[]{:S(2)}, u32[]{:S(2)}) collective-permute-start(bf16[2,64,3,64]{3,1,2,0:T(8,128)(2,1)S(1)} %fusion.163), channel_id=1, source_target_pairs={{30,0},{0,2},{2,4},{4,6},{6,8},{8,10},{10,12},{12,14},{14,16},{16,... | collective-permute-start | bytes 147464 | tf_op jit(solution)/shard_map/while/body/eval_jaxpr/ppermute | solution.py:29
  151.3 14.6 %collective-permute-start = (bf16[2,64,3,64]{3,1,2,0:T(8,128)(2,1)S(1)}, bf16[2,64,3,64]{3,1,2,0:T(8,128)(2,1)S(1)}, u32[]{:S(2)}, u32[]{:S(2)}) collective-permute-start(bf16[2,64,3,64]{3,1,2,0:T(8,128)(2,1)S(1)} %copy.188), channel_id=1, source_target_pairs={{30,0},{0,2},{2,4},{4,6},{6,8},{8,10},{10,12},{12,14},{14,16},{16,... | collective-permute-start | bytes 147464 | tf_op jit(solution)/shard_map/while/body/eval_jaxpr/ppermute | solution.py:29
  151.4 14.5 %collective-permute-start.1 = (bf16[2,64,3,64]{3,1,2,0:T(8,128)(2,1)S(1)}, bf16[2,64,3,64]{3,1,2,0:T(8,128)(2,1)S(1)}, u32[]{:S(2)}, u32[]{:S(2)}) collective-permute-start(bf16[2,64,3,64]{3,1,2,0:T(8,128)(2,1)S(1)} %copy.189), channel_id=1, source_target_pairs={{30,0},{0,2},{2,4},{4,6},{6,8},{8,10},{10,12},{12,14},{14,16},{16,... | collective-permute-start | bytes 147464 | tf_op jit(solution)/shard_map/while/body/eval_jaxpr/ppermute | solution.py:29
  153.8 11.1 %collective-permute-start.3 = (bf16[2,64,3,64]{3,1,2,0:T(8,128)(2,1)S(1)}, bf16[2,64,3,64]{3,1,2,0:T(8,128)(2,1)}, u32[]{:S(2)}, u32[]{:S(2)}) collective-permute-start(bf16[2,64,3,64]{3,1,2,0:T(8,128)(2,1)S(1)} %fusion.163), channel_id=1, source_target_pairs={{30,0},{0,2},{2,4},{4,6},{6,8},{8,10},{10,12},{12,14},{14,16},{16,... | collective-permute-start | bytes 147464 | tf_op jit(solution)/shard_map/while/body/eval_jaxpr/ppermute | solution.py:29
  165.9 15.7 %collective-permute-start = (bf16[2,64,3,64]{3,1,2,0:T(8,128)(2,1)S(1)}, bf16[2,64,3,64]{3,1,2,0:T(8,128)(2,1)S(1)}, u32[]{:S(2)}, u32[]{:S(2)}) collective-permute-start(bf16[2,64,3,64]{3,1,2,0:T(8,128)(2,1)S(1)} %copy.188), channel_id=1, source_target_pairs={{30,0},{0,2},{2,4},{4,6},{6,8},{8,10},{10,12},{12,14},{14,16},{16,... | collective-permute-start | bytes 147464 | tf_op jit(solution)/shard_map/while/body/eval_jaxpr/ppermute | solution.py:29
  166.0 15.7 %collective-permute-start.1 = (bf16[2,64,3,64]{3,1,2,0:T(8,128)(2,1)S(1)}, bf16[2,64,3,64]{3,1,2,0:T(8,128)(2,1)S(1)}, u32[]{:S(2)}, u32[]{:S(2)}) collective-permute-start(bf16[2,64,3,64]{3,1,2,0:T(8,128)(2,1)S(1)} %copy.189), channel_id=1, source_target_pairs={{30,0},{0,2},{2,4},{4,6},{6,8},{8,10},{10,12},{12,14},{14,16},{16,... | collective-permute-start | bytes 147464 | tf_op jit(solution)/shard_map/while/body/eval_jaxpr/ppermute | solution.py:29
  167.6 11.0 %collective-permute-start.2 = (bf16[2,64,3,64]{3,1,2,0:T(8,128)(2,1)S(1)}, bf16[2,64,3,64]{3,1,2,0:T(8,128)(2,1)S(1)}, u32[]{:S(2)}, u32[]{:S(2)}) collective-permute-start(bf16[2,64,3,64]{3,1,2,0:T(8,128)(2,1)S(1)} %fusion.162), channel_id=1, source_target_pairs={{30,0},{0,2},{2,4},{4,6},{6,8},{8,10},{10,12},{12,14},{14,16},{16,... | collective-permute-start | bytes 147464 | tf_op jit(solution)/shard_map/while/body/eval_jaxpr/ppermute | solution.py:29
  167.9 12.8 %collective-permute-start.3 = (bf16[2,64,3,64]{3,1,2,0:T(8,128)(2,1)S(1)}, bf16[2,64,3,64]{3,1,2,0:T(8,128)(2,1)}, u32[]{:S(2)}, u32[]{:S(2)}) collective-permute-start(bf16[2,64,3,64]{3,1,2,0:T(8,128)(2,1)S(1)} %fusion.163), channel_id=1, source_target_pairs={{30,0},{0,2},{2,4},{4,6},{6,8},{8,10},{10,12},{12,14},{14,16},{16,... | collective-permute-start | bytes 147464 | tf_op jit(solution)/shard_map/while/body/eval_jaxpr/ppermute | solution.py:29
  181.7 16.4 %collective-permute-start = (bf16[2,64,3,64]{3,1,2,0:T(8,128)(2,1)S(1)}, bf16[2,64,3,64]{3,1,2,0:T(8,128)(2,1)S(1)}, u32[]{:S(2)}, u32[]{:S(2)}) collective-permute-start(bf16[2,64,3,64]{3,1,2,0:T(8,128)(2,1)S(1)} %copy.188), channel_id=1, source_target_pairs={{30,0},{0,2},{2,4},{4,6},{6,8},{8,10},{10,12},{12,14},{14,16},{16,... | collective-permute-start | bytes 147464 | tf_op jit(solution)/shard_map/while/body/eval_jaxpr/ppermute | solution.py:29
  181.8 16.4 %collective-permute-start.1 = (bf16[2,64,3,64]{3,1,2,0:T(8,128)(2,1)S(1)}, bf16[2,64,3,64]{3,1,2,0:T(8,128)(2,1)S(1)}, u32[]{:S(2)}, u32[]{:S(2)}) collective-permute-start(bf16[2,64,3,64]{3,1,2,0:T(8,128)(2,1)S(1)} %copy.189), channel_id=1, source_target_pairs={{30,0},{0,2},{2,4},{4,6},{6,8},{8,10},{10,12},{12,14},{14,16},{16,... | collective-permute-start | bytes 147464 | tf_op jit(solution)/shard_map/while/body/eval_jaxpr/ppermute | solution.py:29
  183.1 12.1 %collective-permute-start.2 = (bf16[2,64,3,64]{3,1,2,0:T(8,128)(2,1)S(1)}, bf16[2,64,3,64]{3,1,2,0:T(8,128)(2,1)S(1)}, u32[]{:S(2)}, u32[]{:S(2)}) collective-permute-start(bf16[2,64,3,64]{3,1,2,0:T(8,128)(2,1)S(1)} %fusion.162), channel_id=1, source_target_pairs={{30,0},{0,2},{2,4},{4,6},{6,8},{8,10},{10,12},{12,14},{14,16},{16,... | collective-permute-start | bytes 147464 | tf_op jit(solution)/shard_map/while/body/eval_jaxpr/ppermute | solution.py:29
  183.4 13.8 %collective-permute-start.3 = (bf16[2,64,3,64]{3,1,2,0:T(8,128)(2,1)S(1)}, bf16[2,64,3,64]{3,1,2,0:T(8,128)(2,1)}, u32[]{:S(2)}, u32[]{:S(2)}) collective-permute-start(bf16[2,64,3,64]{3,1,2,0:T(8,128)(2,1)S(1)} %fusion.163), channel_id=1, source_target_pairs={{30,0},{0,2},{2,4},{4,6},{6,8},{8,10},{10,12},{12,14},{14,16},{16,... | collective-permute-start | bytes 147464 | tf_op jit(solution)/shard_map/while/body/eval_jaxpr/ppermute | solution.py:29
  198.2 15.6 %collective-permute-start = (bf16[2,64,3,64]{3,1,2,0:T(8,128)(2,1)S(1)}, bf16[2,64,3,64]{3,1,2,0:T(8,128)(2,1)S(1)}, u32[]{:S(2)}, u32[]{:S(2)}) collective-permute-start(bf16[2,64,3,64]{3,1,2,0:T(8,128)(2,1)S(1)} %copy.188), channel_id=1, source_target_pairs={{30,0},{0,2},{2,4},{4,6},{6,8},{8,10},{10,12},{12,14},{14,16},{16,... | collective-permute-start | bytes 147464 | tf_op jit(solution)/shard_map/while/body/eval_jaxpr/ppermute | solution.py:29
  198.3 15.5 %collective-permute-start.1 = (bf16[2,64,3,64]{3,1,2,0:T(8,128)(2,1)S(1)}, bf16[2,64,3,64]{3,1,2,0:T(8,128)(2,1)S(1)}, u32[]{:S(2)}, u32[]{:S(2)}) collective-permute-start(bf16[2,64,3,64]{3,1,2,0:T(8,128)(2,1)S(1)} %copy.189), channel_id=1, source_target_pairs={{30,0},{0,2},{2,4},{4,6},{6,8},{8,10},{10,12},{12,14},{14,16},{16,... | collective-permute-start | bytes 147464 | tf_op jit(solution)/shard_map/while/body/eval_jaxpr/ppermute | solution.py:29
  199.6 12.1 %collective-permute-start.2 = (bf16[2,64,3,64]{3,1,2,0:T(8,128)(2,1)S(1)}, bf16[2,64,3,64]{3,1,2,0:T(8,128)(2,1)S(1)}, u32[]{:S(2)}, u32[]{:S(2)}) collective-permute-start(bf16[2,64,3,64]{3,1,2,0:T(8,128)(2,1)S(1)} %fusion.162), channel_id=1, source_target_pairs={{30,0},{0,2},{2,4},{4,6},{6,8},{8,10},{10,12},{12,14},{14,16},{16,... | collective-permute-start | bytes 147464 | tf_op jit(solution)/shard_map/while/body/eval_jaxpr/ppermute | solution.py:29
  199.9 12.9 %collective-permute-start.3 = (bf16[2,64,3,64]{3,1,2,0:T(8,128)(2,1)S(1)}, bf16[2,64,3,64]{3,1,2,0:T(8,128)(2,1)}, u32[]{:S(2)}, u32[]{:S(2)}) collective-permute-start(bf16[2,64,3,64]{3,1,2,0:T(8,128)(2,1)S(1)} %fusion.163), channel_id=1, source_target_pairs={{30,0},{0,2},{2,4},{4,6},{6,8},{8,10},{10,12},{12,14},{14,16},{16,... | collective-permute-start | bytes 147464 | tf_op jit(solution)/shard_map/while/body/eval_jaxpr/ppermute | solution.py:29
  213.8 14.6 %collective-permute-start = (bf16[2,64,3,64]{3,1,2,0:T(8,128)(2,1)S(1)}, bf16[2,64,3,64]{3,1,2,0:T(8,128)(2,1)S(1)}, u32[]{:S(2)}, u32[]{:S(2)}) collective-permute-start(bf16[2,64,3,64]{3,1,2,0:T(8,128)(2,1)S(1)} %copy.188), channel_id=1, source_target_pairs={{30,0},{0,2},{2,4},{4,6},{6,8},{8,10},{10,12},{12,14},{14,16},{16,... | collective-permute-start | bytes 147464 | tf_op jit(solution)/shard_map/while/body/eval_jaxpr/ppermute | solution.py:29
  213.9 14.5 %collective-permute-start.1 = (bf16[2,64,3,64]{3,1,2,0:T(8,128)(2,1)S(1)}, bf16[2,64,3,64]{3,1,2,0:T(8,128)(2,1)S(1)}, u32[]{:S(2)}, u32[]{:S(2)}) collective-permute-start(bf16[2,64,3,64]{3,1,2,0:T(8,128)(2,1)S(1)} %copy.189), channel_id=1, source_target_pairs={{30,0},{0,2},{2,4},{4,6},{6,8},{8,10},{10,12},{12,14},{14,16},{16,... | collective-permute-start | bytes 147464 | tf_op jit(solution)/shard_map/while/body/eval_jaxpr/ppermute | solution.py:29
  215.2 11.1 %collective-permute-start.2 = (bf16[2,64,3,64]{3,1,2,0:T(8,128)(2,1)S(1)}, bf16[2,64,3,64]{3,1,2,0:T(8,128)(2,1)S(1)}, u32[]{:S(2)}, u32[]{:S(2)}) collective-permute-start(bf16[2,64,3,64]{3,1,2,0:T(8,128)(2,1)S(1)} %fusion.162), channel_id=1, source_target_pairs={{30,0},{0,2},{2,4},{4,6},{6,8},{8,10},{10,12},{12,14},{14,16},{16,... | collective-permute-start | bytes 147464 | tf_op jit(solution)/shard_map/while/body/eval_jaxpr/ppermute | solution.py:29
  215.5 12.0 %collective-permute-start.3 = (bf16[2,64,3,64]{3,1,2,0:T(8,128)(2,1)S(1)}, bf16[2,64,3,64]{3,1,2,0:T(8,128)(2,1)}, u32[]{:S(2)}, u32[]{:S(2)}) collective-permute-start(bf16[2,64,3,64]{3,1,2,0:T(8,128)(2,1)S(1)} %fusion.163), channel_id=1, source_target_pairs={{30,0},{0,2},{2,4},{4,6},{6,8},{8,10},{10,12},{12,14},{14,16},{16,... | collective-permute-start | bytes 147464 | tf_op jit(solution)/shard_map/while/body/eval_jaxpr/ppermute | solution.py:29
  228.5 13.6 %collective-permute-start = (bf16[2,64,3,64]{3,1,2,0:T(8,128)(2,1)S(1)}, bf16[2,64,3,64]{3,1,2,0:T(8,128)(2,1)S(1)}, u32[]{:S(2)}, u32[]{:S(2)}) collective-permute-start(bf16[2,64,3,64]{3,1,2,0:T(8,128)(2,1)S(1)} %copy.188), channel_id=1, source_target_pairs={{30,0},{0,2},{2,4},{4,6},{6,8},{8,10},{10,12},{12,14},{14,16},{16,... | collective-permute-start | bytes 147464 | tf_op jit(solution)/shard_map/while/body/eval_jaxpr/ppermute | solution.py:29
  228.5 13.5 %collective-permute-start.1 = (bf16[2,64,3,64]{3,1,2,0:T(8,128)(2,1)S(1)}, bf16[2,64,3,64]{3,1,2,0:T(8,128)(2,1)S(1)}, u32[]{:S(2)}, u32[]{:S(2)}) collective-permute-start(bf16[2,64,3,64]{3,1,2,0:T(8,128)(2,1)S(1)} %copy.189), channel_id=1, source_target_pairs={{30,0},{0,2},{2,4},{4,6},{6,8},{8,10},{10,12},{12,14},{14,16},{16,... | collective-permute-start | bytes 147464 | tf_op jit(solution)/shard_map/while/body/eval_jaxpr/ppermute | solution.py:29
  229.8 10.1 %collective-permute-start.2 = (bf16[2,64,3,64]{3,1,2,0:T(8,128)(2,1)S(1)}, bf16[2,64,3,64]{3,1,2,0:T(8,128)(2,1)S(1)}, u32[]{:S(2)}, u32[]{:S(2)}) collective-permute-start(bf16[2,64,3,64]{3,1,2,0:T(8,128)(2,1)S(1)} %fusion.162), channel_id=1, source_target_pairs={{30,0},{0,2},{2,4},{4,6},{6,8},{8,10},{10,12},{12,14},{14,16},{16,... | collective-permute-start | bytes 147464 | tf_op jit(solution)/shard_map/while/body/eval_jaxpr/ppermute | solution.py:29
  230.2 10.9 %collective-permute-start.3 = (bf16[2,64,3,64]{3,1,2,0:T(8,128)(2,1)S(1)}, bf16[2,64,3,64]{3,1,2,0:T(8,128)(2,1)}, u32[]{:S(2)}, u32[]{:S(2)}) collective-permute-start(bf16[2,64,3,64]{3,1,2,0:T(8,128)(2,1)S(1)} %fusion.163), channel_id=1, source_target_pairs={{30,0},{0,2},{2,4},{4,6},{6,8},{8,10},{10,12},{12,14},{14,16},{16,... | collective-permute-start | bytes 147464 | tf_op jit(solution)/shard_map/while/body/eval_jaxpr/ppermute | solution.py:29
  242.1 12.5 %collective-permute-start = (bf16[2,64,3,64]{3,1,2,0:T(8,128)(2,1)S(1)}, bf16[2,64,3,64]{3,1,2,0:T(8,128)(2,1)S(1)}, u32[]{:S(2)}, u32[]{:S(2)}) collective-permute-start(bf16[2,64,3,64]{3,1,2,0:T(8,128)(2,1)S(1)} %copy.188), channel_id=1, source_target_pairs={{30,0},{0,2},{2,4},{4,6},{6,8},{8,10},{10,12},{12,14},{14,16},{16,... | collective-permute-start | bytes 147464 | tf_op jit(solution)/shard_map/while/body/eval_jaxpr/ppermute | solution.py:29
  242.2 12.5 %collective-permute-start.1 = (bf16[2,64,3,64]{3,1,2,0:T(8,128)(2,1)S(1)}, bf16[2,64,3,64]{3,1,2,0:T(8,128)(2,1)S(1)}, u32[]{:S(2)}, u32[]{:S(2)}) collective-permute-start(bf16[2,64,3,64]{3,1,2,0:T(8,128)(2,1)S(1)} %copy.189), channel_id=1, source_target_pairs={{30,0},{0,2},{2,4},{4,6},{6,8},{8,10},{10,12},{12,14},{14,16},{16,... | collective-permute-start | bytes 147464 | tf_op jit(solution)/shard_map/while/body/eval_jaxpr/ppermute | solution.py:29
  243.8 9.9 %collective-permute-start.3 = (bf16[2,64,3,64]{3,1,2,0:T(8,128)(2,1)S(1)}, bf16[2,64,3,64]{3,1,2,0:T(8,128)(2,1)}, u32[]{:S(2)}, u32[]{:S(2)}) collective-permute-start(bf16[2,64,3,64]{3,1,2,0:T(8,128)(2,1)S(1)} %fusion.163), channel_id=1, source_target_pairs={{30,0},{0,2},{2,4},{4,6},{6,8},{8,10},{10,12},{12,14},{14,16},{16,... | collective-permute-start | bytes 147464 | tf_op jit(solution)/shard_map/while/body/eval_jaxpr/ppermute | solution.py:29
  254.7 12.4 %collective-permute-start = (bf16[2,64,3,64]{3,1,2,0:T(8,128)(2,1)S(1)}, bf16[2,64,3,64]{3,1,2,0:T(8,128)(2,1)S(1)}, u32[]{:S(2)}, u32[]{:S(2)}) collective-permute-start(bf16[2,64,3,64]{3,1,2,0:T(8,128)(2,1)S(1)} %copy.188), channel_id=1, source_target_pairs={{30,0},{0,2},{2,4},{4,6},{6,8},{8,10},{10,12},{12,14},{14,16},{16,... | collective-permute-start | bytes 147464 | tf_op jit(solution)/shard_map/while/body/eval_jaxpr/ppermute | solution.py:29
  254.8 12.4 %collective-permute-start.1 = (bf16[2,64,3,64]{3,1,2,0:T(8,128)(2,1)S(1)}, bf16[2,64,3,64]{3,1,2,0:T(8,128)(2,1)S(1)}, u32[]{:S(2)}, u32[]{:S(2)}) collective-permute-start(bf16[2,64,3,64]{3,1,2,0:T(8,128)(2,1)S(1)} %copy.189), channel_id=1, source_target_pairs={{30,0},{0,2},{2,4},{4,6},{6,8},{8,10},{10,12},{12,14},{14,16},{16,... | collective-permute-start | bytes 147464 | tf_op jit(solution)/shard_map/while/body/eval_jaxpr/ppermute | solution.py:29
  256.4 9.8 %collective-permute-start.3 = (bf16[2,64,3,64]{3,1,2,0:T(8,128)(2,1)S(1)}, bf16[2,64,3,64]{3,1,2,0:T(8,128)(2,1)}, u32[]{:S(2)}, u32[]{:S(2)}) collective-permute-start(bf16[2,64,3,64]{3,1,2,0:T(8,128)(2,1)S(1)} %fusion.163), channel_id=1, source_target_pairs={{30,0},{0,2},{2,4},{4,6},{6,8},{8,10},{10,12},{12,14},{14,16},{16,... | collective-permute-start | bytes 147464 | tf_op jit(solution)/shard_map/while/body/eval_jaxpr/ppermute | solution.py:29
  267.2 12.4 %collective-permute-start = (bf16[2,64,3,64]{3,1,2,0:T(8,128)(2,1)S(1)}, bf16[2,64,3,64]{3,1,2,0:T(8,128)(2,1)S(1)}, u32[]{:S(2)}, u32[]{:S(2)}) collective-permute-start(bf16[2,64,3,64]{3,1,2,0:T(8,128)(2,1)S(1)} %copy.188), channel_id=1, source_target_pairs={{30,0},{0,2},{2,4},{4,6},{6,8},{8,10},{10,12},{12,14},{14,16},{16,... | collective-permute-start | bytes 147464 | tf_op jit(solution)/shard_map/while/body/eval_jaxpr/ppermute | solution.py:29
  267.3 12.4 %collective-permute-start.1 = (bf16[2,64,3,64]{3,1,2,0:T(8,128)(2,1)S(1)}, bf16[2,64,3,64]{3,1,2,0:T(8,128)(2,1)S(1)}, u32[]{:S(2)}, u32[]{:S(2)}) collective-permute-start(bf16[2,64,3,64]{3,1,2,0:T(8,128)(2,1)S(1)} %copy.189), channel_id=1, source_target_pairs={{30,0},{0,2},{2,4},{4,6},{6,8},{8,10},{10,12},{12,14},{14,16},{16,... | collective-permute-start | bytes 147464 | tf_op jit(solution)/shard_map/while/body/eval_jaxpr/ppermute | solution.py:29
  268.9 9.8 %collective-permute-start.3 = (bf16[2,64,3,64]{3,1,2,0:T(8,128)(2,1)S(1)}, bf16[2,64,3,64]{3,1,2,0:T(8,128)(2,1)}, u32[]{:S(2)}, u32[]{:S(2)}) collective-permute-start(bf16[2,64,3,64]{3,1,2,0:T(8,128)(2,1)S(1)} %fusion.163), channel_id=1, source_target_pairs={{30,0},{0,2},{2,4},{4,6},{6,8},{8,10},{10,12},{12,14},{14,16},{16,... | collective-permute-start | bytes 147464 | tf_op jit(solution)/shard_map/while/body/eval_jaxpr/ppermute | solution.py:29
  279.7 14.5 %collective-permute-start = (bf16[2,64,3,64]{3,1,2,0:T(8,128)(2,1)S(1)}, bf16[2,64,3,64]{3,1,2,0:T(8,128)(2,1)S(1)}, u32[]{:S(2)}, u32[]{:S(2)}) collective-permute-start(bf16[2,64,3,64]{3,1,2,0:T(8,128)(2,1)S(1)} %copy.188), channel_id=1, source_target_pairs={{30,0},{0,2},{2,4},{4,6},{6,8},{8,10},{10,12},{12,14},{14,16},{16,... | collective-permute-start | bytes 147464 | tf_op jit(solution)/shard_map/while/body/eval_jaxpr/ppermute | solution.py:29
  279.8 14.5 %collective-permute-start.1 = (bf16[2,64,3,64]{3,1,2,0:T(8,128)(2,1)S(1)}, bf16[2,64,3,64]{3,1,2,0:T(8,128)(2,1)S(1)}, u32[]{:S(2)}, u32[]{:S(2)}) collective-permute-start(bf16[2,64,3,64]{3,1,2,0:T(8,128)(2,1)S(1)} %copy.189), channel_id=1, source_target_pairs={{30,0},{0,2},{2,4},{4,6},{6,8},{8,10},{10,12},{12,14},{14,16},{16,... | collective-permute-start | bytes 147464 | tf_op jit(solution)/shard_map/while/body/eval_jaxpr/ppermute | solution.py:29
  294.3 16.6 %collective-permute-start = (bf16[2,64,3,64]{3,1,2,0:T(8,128)(2,1)S(1)}, bf16[2,64,3,64]{3,1,2,0:T(8,128)(2,1)S(1)}, u32[]{:S(2)}, u32[]{:S(2)}) collective-permute-start(bf16[2,64,3,64]{3,1,2,0:T(8,128)(2,1)S(1)} %copy.188), channel_id=1, source_target_pairs={{30,0},{0,2},{2,4},{4,6},{6,8},{8,10},{10,12},{12,14},{14,16},{16,... | collective-permute-start | bytes 147464 | tf_op jit(solution)/shard_map/while/body/eval_jaxpr/ppermute | solution.py:29
  294.4 16.6 %collective-permute-start.1 = (bf16[2,64,3,64]{3,1,2,0:T(8,128)(2,1)S(1)}, bf16[2,64,3,64]{3,1,2,0:T(8,128)(2,1)S(1)}, u32[]{:S(2)}, u32[]{:S(2)}) collective-permute-start(bf16[2,64,3,64]{3,1,2,0:T(8,128)(2,1)S(1)} %copy.189), channel_id=1, source_target_pairs={{30,0},{0,2},{2,4},{4,6},{6,8},{8,10},{10,12},{12,14},{14,16},{16,... | collective-permute-start | bytes 147464 | tf_op jit(solution)/shard_map/while/body/eval_jaxpr/ppermute | solution.py:29
  298.4 9.4 %collective-permute-start.2 = (bf16[2,64,3,64]{3,1,2,0:T(8,128)(2,1)S(1)}, bf16[2,64,3,64]{3,1,2,0:T(8,128)(2,1)S(1)}, u32[]{:S(2)}, u32[]{:S(2)}) collective-permute-start(bf16[2,64,3,64]{3,1,2,0:T(8,128)(2,1)S(1)} %fusion.162), channel_id=1, source_target_pairs={{30,0},{0,2},{2,4},{4,6},{6,8},{8,10},{10,12},{12,14},{14,16},{16,... | collective-permute-start | bytes 147464 | tf_op jit(solution)/shard_map/while/body/eval_jaxpr/ppermute | solution.py:29
  299.2 10.8 %collective-permute-start.3 = (bf16[2,64,3,64]{3,1,2,0:T(8,128)(2,1)S(1)}, bf16[2,64,3,64]{3,1,2,0:T(8,128)(2,1)}, u32[]{:S(2)}, u32[]{:S(2)}) collective-permute-start(bf16[2,64,3,64]{3,1,2,0:T(8,128)(2,1)S(1)} %fusion.163), channel_id=1, source_target_pairs={{30,0},{0,2},{2,4},{4,6},{6,8},{8,10},{10,12},{12,14},{14,16},{16,... | collective-permute-start | bytes 147464 | tf_op jit(solution)/shard_map/while/body/eval_jaxpr/ppermute | solution.py:29
  311.0 14.6 %collective-permute-start = (bf16[2,64,3,64]{3,1,2,0:T(8,128)(2,1)S(1)}, bf16[2,64,3,64]{3,1,2,0:T(8,128)(2,1)S(1)}, u32[]{:S(2)}, u32[]{:S(2)}) collective-permute-start(bf16[2,64,3,64]{3,1,2,0:T(8,128)(2,1)S(1)} %copy.188), channel_id=1, source_target_pairs={{30,0},{0,2},{2,4},{4,6},{6,8},{8,10},{10,12},{12,14},{14,16},{16,... | collective-permute-start | bytes 147464 | tf_op jit(solution)/shard_map/while/body/eval_jaxpr/ppermute | solution.py:29
  311.1 14.5 %collective-permute-start.1 = (bf16[2,64,3,64]{3,1,2,0:T(8,128)(2,1)S(1)}, bf16[2,64,3,64]{3,1,2,0:T(8,128)(2,1)S(1)}, u32[]{:S(2)}, u32[]{:S(2)}) collective-permute-start(bf16[2,64,3,64]{3,1,2,0:T(8,128)(2,1)S(1)} %copy.189), channel_id=1, source_target_pairs={{30,0},{0,2},{2,4},{4,6},{6,8},{8,10},{10,12},{12,14},{14,16},{16,... | collective-permute-start | bytes 147464 | tf_op jit(solution)/shard_map/while/body/eval_jaxpr/ppermute | solution.py:29
  312.4 11.1 %collective-permute-start.2 = (bf16[2,64,3,64]{3,1,2,0:T(8,128)(2,1)S(1)}, bf16[2,64,3,64]{3,1,2,0:T(8,128)(2,1)S(1)}, u32[]{:S(2)}, u32[]{:S(2)}) collective-permute-start(bf16[2,64,3,64]{3,1,2,0:T(8,128)(2,1)S(1)} %fusion.162), channel_id=1, source_target_pairs={{30,0},{0,2},{2,4},{4,6},{6,8},{8,10},{10,12},{12,14},{14,16},{16,... | collective-permute-start | bytes 147464 | tf_op jit(solution)/shard_map/while/body/eval_jaxpr/ppermute | solution.py:29
  312.8 11.8 %collective-permute-start.3 = (bf16[2,64,3,64]{3,1,2,0:T(8,128)(2,1)S(1)}, bf16[2,64,3,64]{3,1,2,0:T(8,128)(2,1)}, u32[]{:S(2)}, u32[]{:S(2)}) collective-permute-start(bf16[2,64,3,64]{3,1,2,0:T(8,128)(2,1)S(1)} %fusion.163), channel_id=1, source_target_pairs={{30,0},{0,2},{2,4},{4,6},{6,8},{8,10},{10,12},{12,14},{14,16},{16,... | collective-permute-start | bytes 147464 | tf_op jit(solution)/shard_map/while/body/eval_jaxpr/ppermute | solution.py:29
  325.6 12.4 %collective-permute-start = (bf16[2,64,3,64]{3,1,2,0:T(8,128)(2,1)S(1)}, bf16[2,64,3,64]{3,1,2,0:T(8,128)(2,1)S(1)}, u32[]{:S(2)}, u32[]{:S(2)}) collective-permute-start(bf16[2,64,3,64]{3,1,2,0:T(8,128)(2,1)S(1)} %copy.188), channel_id=1, source_target_pairs={{30,0},{0,2},{2,4},{4,6},{6,8},{8,10},{10,12},{12,14},{14,16},{16,... | collective-permute-start | bytes 147464 | tf_op jit(solution)/shard_map/while/body/eval_jaxpr/ppermute | solution.py:29
  325.7 12.4 %collective-permute-start.1 = (bf16[2,64,3,64]{3,1,2,0:T(8,128)(2,1)S(1)}, bf16[2,64,3,64]{3,1,2,0:T(8,128)(2,1)S(1)}, u32[]{:S(2)}, u32[]{:S(2)}) collective-permute-start(bf16[2,64,3,64]{3,1,2,0:T(8,128)(2,1)S(1)} %copy.189), channel_id=1, source_target_pairs={{30,0},{0,2},{2,4},{4,6},{6,8},{8,10},{10,12},{12,14},{14,16},{16,... | collective-permute-start | bytes 147464 | tf_op jit(solution)/shard_map/while/body/eval_jaxpr/ppermute | solution.py:29
  327.3 9.8 %collective-permute-start.3 = (bf16[2,64,3,64]{3,1,2,0:T(8,128)(2,1)S(1)}, bf16[2,64,3,64]{3,1,2,0:T(8,128)(2,1)}, u32[]{:S(2)}, u32[]{:S(2)}) collective-permute-start(bf16[2,64,3,64]{3,1,2,0:T(8,128)(2,1)S(1)} %fusion.163), channel_id=1, source_target_pairs={{30,0},{0,2},{2,4},{4,6},{6,8},{8,10},{10,12},{12,14},{14,16},{16,... | collective-permute-start | bytes 147464 | tf_op jit(solution)/shard_map/while/body/eval_jaxpr/ppermute | solution.py:29
  340.1 10.0 %collective-permute-start.8 = (bf16[2,64,3,64]{1,3,2,0:T(8,128)(2,1)S(1)}, bf16[2,64,3,64]{1,3,2,0:T(8,128)(2,1)S(1)}, u32[]{:S(2)}, u32[]{:S(2)}) collective-permute-start(bf16[2,64,3,64]{1,3,2,0:T(8,128)(2,1)S(1)} %fusion.37), channel_id=1, source_target_pairs={{30,0},{0,2},{2,4},{4,6},{6,8},{8,10},{10,12},{12,14},{14,16},{16,... | collective-permute-start | bytes 147464 | tf_op jit(solution)/shard_map/ppermute | solution.py:29
  350.1 14.7 %reduce-scatter.10.cloned.1.call-start = ((), (), s32[]{:S(2)}) async-start(), calls=%async_computation.11 | async-start | bytes 442368 | tf_op jit(solution)/shard_map/reduce_scatter | solution.py:326
  351.5 24.7 %reduce-scatter.14.cloned.1.call-start = ((), (), s32[]{:S(2)}) async-start(), calls=%async_computation.13 | async-start | bytes 1105920 | tf_op jit(solution)/shard_map/reduce_scatter | solution.py:332
  353.1 35.4 %reduce-scatter.8.cloned.1.call-start = ((), (), s32[]{:S(2)}) async-start(), calls=%async_computation.10 | async-start | bytes 1105920 | tf_op jit(solution)/shard_map/reduce_scatter | solution.py:323
  355.6 46.2 %reduce-scatter.18.cloned.1.call-start = ((), (), s32[]{:S(2)}) async-start(), calls=%async_computation.15 | async-start | bytes 2654208 | tf_op jit(solution)/shard_map/reduce_scatter | solution.py:341
  357.5 57.7 %reduce-scatter.16.cloned.1.call-start = ((), (), s32[]{:S(2)}) async-start(), calls=%async_computation.14 | async-start | bytes 2654208 | tf_op jit(solution)/shard_map/reduce_scatter | solution.py:338
  359.4 69.0 %reduce-scatter.20.cloned.1.call-start = ((), (), s32[]{:S(2)}) async-start(), calls=%async_computation.16 | async-start | bytes 2654208 | tf_op jit(solution)/shard_map/reduce_scatter | solution.py:344
  361.4 238.1 %all-reduce.10.cloned.1.call-start = ((), (), s32[]{:S(2)}) async-start(), calls=%async_computation.17 | async-start | bytes 7372800 | tf_op jit(solution)/shard_map/psum | solution.py:352
  (73 other events, 655.9 us)
Sparse Core Ops, SparseCore 0:
  9.6 13.3 all-gather.3
  24.5 10.8 all-gather.5
  37.0 11.2 all-gather.7
  350.2 3.5 reduce-scatter.11
  355.9 8.8 reduce-scatter.9
  366.9 9.3 reduce-scatter.13
  379.1 9.3 reduce-scatter.7
  391.3 10.4 reduce-scatter.17
  404.8 10.4 reduce-scatter.15
  417.9 10.4 reduce-scatter.19
  436.0 163.4 all-reduce.9
